TPU v7x, 512 devices: a whole 4x4x16 slice. The times are simulated.
512 devices in a mesh: seq: 16 (over y_lo, x, core), pair: 32 (over y_hi, z).
Axes of the slice: x: 4, y: 4 (y_hi: 2, y_lo: 2; y = y_hi * 2 + y_lo), z: 16, core: 2. Of those that a mesh axis runs over, the one named last changes fastest.
Arguments:
- queries: bfloat16 [32, 2048, 1792], P('pair', 'seq'), may hold values from -6 to 6
- keys_values: bfloat16 [32, 2048, 512], P('pair', 'seq'), may hold values from -6 to 6
- cotangent: bfloat16 [32, 2048, 1792], P('pair', 'seq'), may hold values from -6 to 6
- resp_len: int32 [32, 2], P('pair'), may hold values from 128 to 512, as said below
- query_bias: float32 [1792], replicated, may hold values from -3 to 3
Outputs:
- grad_queries: float32 [32, 2048, 1792], P('pair', 'seq')
- grad_keys_values: float32 [32, 2048, 512], P('pair', 'seq')
- grad_bias_q: float32 [1792], replicated
- grad_bias_v: float32 [256], replicated
Inputs may be any that keep to these rules, and one draw needn't show every extreme that they name: `resp_len`: in every pair one of the two lengths equals 512.
All inputs are finite; a program needn't handle non-finite values.
Results may differ from a plain program's by a relative error of at most 0.035.
Values may be sent and summed in bfloat16 or wider, within the bound.
A program may use at most 64 MiB of HBM per device.

v0:
```python
import math

import jax
import jax.numpy as jnp
from jax import lax
from jax.sharding import PartitionSpec as P

P_DEV = 64
R_DEV = 32
QUERY_HEADS = 14
KEY_VALUE_HEADS = 2
HEAD_SIZE = 128


def passed_along(shard, axis, by):
    count = lax.axis_size(axis)
    return lax.ppermute(shard, axis, [(i, (i + by) % count) for i in range(count)])


def row_layout(row_block, prompt_dev, resp_dev):
    window_length = prompt_dev + 2 * resp_dev
    block_tile = row_block // window_length
    offset = row_block % window_length
    kind = jnp.where(
        offset < prompt_dev, 0, jnp.where(offset < prompt_dev + resp_dev, 1, 2)
    ).astype(jnp.int32)
    place = jnp.where(
        kind == 0,
        block_tile * prompt_dev + offset,
        block_tile * resp_dev + offset - prompt_dev - (kind - 1) * resp_dev,
    )
    return (kind, place)


def visible(q_kind, q_place, k_kind, k_place, lengths):
    k_limit = jnp.where(k_kind == 1, lengths[0], lengths[1])
    causal = k_place <= q_place
    from_prompt = (k_kind == 0) & ((q_kind != 0) | causal)
    from_reply = (k_kind == q_kind) & (k_kind != 0) & causal & (k_place < k_limit)
    return from_prompt | from_reply


def live_rows(kind, place, lengths):
    limit = jnp.where(kind == 1, lengths[0], lengths[1])
    return (kind == 0) | (place < limit)


def split_kv(block_tile):
    row_count = block_tile.shape[0]
    return (
        block_tile[:, : KEY_VALUE_HEADS * HEAD_SIZE].reshape(row_count, KEY_VALUE_HEADS, HEAD_SIZE),
        block_tile[:, KEY_VALUE_HEADS * HEAD_SIZE :].reshape(row_count, KEY_VALUE_HEADS, HEAD_SIZE),
    )


def on_device(queries, keys_values, cotangent, resp_len, query_bias):
    query_group = QUERY_HEADS // KEY_VALUE_HEADS
    scale = 1.0 / math.sqrt(HEAD_SIZE)
    member = lax.axis_index("seq")
    cycle_size = lax.axis_size("seq")
    window_length = queries.shape[1]
    lengths = resp_len[0]
    q_index = member * window_length + jnp.arange(window_length, dtype=jnp.int32)
    q_kind, q_place = row_layout(q_index, P_DEV, R_DEV)
    q_live = live_rows(q_kind, q_place, lengths)
    query_head_rows = (
        (queries[0].astype(jnp.float32) + query_bias)
        .astype(jnp.bfloat16)
        .reshape(window_length, KEY_VALUE_HEADS, query_group, HEAD_SIZE)
    )
    kv_local = keys_values[0]

    def block_mask(start, row_count):
        k_index = start + jnp.arange(row_count, dtype=jnp.int32)
        k_kind, k_place = row_layout(k_index, P_DEV, R_DEV)
        allow = visible(
            q_kind[:, None], q_place[:, None], k_kind[None, :], k_place[None, :], lengths
        )
        return allow[:, None, None, :]

    def block_scores(key_rows, start, row_count):
        allow = block_mask(start, row_count)
        scores = (
            jnp.einsum(
                "qhgd,khd->qhgk", query_head_rows, key_rows, preferred_element_type=jnp.float32
            )
            * scale
        )
        return (allow, jnp.where(allow, scores, jnp.float32(-1e30)))

    piece = lax.all_gather(kv_local, "seq", axis=0, tiled=True)
    forward_top = jnp.full((window_length, KEY_VALUE_HEADS, query_group), -1e30, jnp.float32)
    key_rows, value_rows = split_kv(piece)
    allow, scores = block_scores(key_rows, jnp.int32(0), piece.shape[0])
    new_top = jnp.maximum(forward_top, scores.max(-1))
    expo = jnp.where(allow, jnp.exp(scores - new_top[..., None]), jnp.float32(0.0))
    forward_total = expo.sum(-1)
    acc = jnp.einsum(
        "qhgk,khd->qhgd", expo.astype(jnp.bfloat16), value_rows, preferred_element_type=jnp.float32
    )
    top, total, acc = (new_top, forward_total, acc)
    attended = (acc / total[..., None]).astype(jnp.bfloat16)
    output_gradient = jnp.where(
        q_live[:, None], cotangent[0], jnp.zeros_like(cotangent[0])
    ).reshape(window_length, KEY_VALUE_HEADS, query_group, HEAD_SIZE)
    row_dot = jnp.sum(output_gradient.astype(jnp.float32) * attended.astype(jnp.float32), -1)

    def backward_block(block_tile, start, dq_acc):
        key_rows, value_rows = split_kv(block_tile)
        row_count = block_tile.shape[0]
        allow, scores = block_scores(key_rows, start, row_count)
        prob = jnp.where(
            allow, jnp.exp(scores - top[..., None]) / total[..., None], jnp.float32(0.0)
        )
        value_gradient = jnp.einsum(
            "njma,njmv->ajv",
            prob.astype(jnp.bfloat16),
            output_gradient,
            preferred_element_type=jnp.float32,
        )
        grad_prob = jnp.einsum(
            "qhgd,khd->qhgk", output_gradient, value_rows, preferred_element_type=jnp.float32
        )
        score_gradient = (prob * (grad_prob - row_dot[..., None]) * scale).astype(jnp.bfloat16)
        dq_acc = dq_acc + jnp.einsum(
            "qhgk,khd->qhgd", score_gradient, key_rows, preferred_element_type=jnp.float32
        )
        key_gradient = jnp.einsum(
            "njma,njmv->ajv", score_gradient, query_head_rows, preferred_element_type=jnp.float32
        )
        return (
            dq_acc,
            jnp.concatenate(
                [
                    key_gradient.reshape(row_count, KEY_VALUE_HEADS * HEAD_SIZE),
                    value_gradient.reshape(row_count, KEY_VALUE_HEADS * HEAD_SIZE),
                ],
                1,
            ),
        )

    query_gradient_begin = jnp.zeros(
        (window_length, KEY_VALUE_HEADS, query_group, HEAD_SIZE), jnp.float32
    )
    gradient_begin = jnp.zeros((window_length, 2 * KEY_VALUE_HEADS * HEAD_SIZE), jnp.float32)

    def rotate_step(step, carry):
        block_tile, grads, dq_acc = carry
        source = (member - step) % cycle_size
        dq_acc, contrib = backward_block(block_tile, source * window_length, dq_acc)
        block_tile = passed_along(block_tile, "seq", 1)
        grads = passed_along((grads + contrib).astype(jnp.bfloat16), "seq", 1).astype(jnp.float32)
        return (block_tile, grads, dq_acc)

    block_end, grads, dq_acc = lax.fori_loop(
        0, cycle_size, rotate_step, (kv_local, gradient_begin, query_gradient_begin)
    )
    grad_q = dq_acc.reshape(window_length, QUERY_HEADS * HEAD_SIZE)
    total_q, total_v = lax.psum(
        (grad_q.sum(0), grads[:, KEY_VALUE_HEADS * HEAD_SIZE :].sum(0)), ("seq", "pair")
    )
    return (grad_q[None], grads[None], total_q, total_v)


def solution(mesh):
    return jax.shard_map(
        on_device,
        mesh=mesh,
        in_specs=(
            P("pair", "seq", None),
            P("pair", "seq", None),
            P("pair", "seq", None),
            P("pair", None),
            P(),
        ),
        out_specs=(P("pair", "seq", None), P("pair", "seq", None), P(), P()),
        check_vma=False,
    )
```

profile of v0, /device:TPU:1, one launch (start us, length us, event | category | flops | bytes accessed | tf_op | source)
XLA Modules:
  0.0 420.6 jit_solution(5719479540047305322)
XLA Ops:
  7.2 1.7 copy.28
  12.2 1.3 fusion.71
  16.9 44.6 %all-gather.3.cloned.1.call-done = bf16[1,2048,512]{1,2,0:T(8,128)(2,1)} async-done(((bf16[1,128,512]{1,2,0:T(8,128)(2,1)}), bf16[1,2048,512]{1,2,0:T(8,128)(2,1)}) %all-gather.3.cloned.1.call-update) | async-done | bytes 2097168 | tf_op jit(solution)/shard_map/all_gather | solution.py:91
  61.5 1.7 fusion.70
  63.2 2.7 bitcast_reduce_fusion
  66.0 5.2 %copy-done = f32[2,128,7,2048]{3,1,2,0:T(8,128)} copy-done((f32[2,128,7,2048]{3,1,2,0:T(8,128)}, f32[2,128,7,2048]{3,1,2,0:T(8,128)S(1)}, u32[]{:S(2)}) %copy-start) | copy-done | bytes 14680088
  71.2 4.7 %fusion.25 = f32[128,2,7]{0,2,1:T(8,128)S(1)} fusion(f32[2,128,7,2048]{3,1,2,0:T(8,128)S(1)} %get-tuple-element.517, f32[128,2,7]{0,2,1:T(8,128)S(1)} %broadcast_maximum_fusion, pred[128,2048]{1,0:T(8,128)(4,1)S(1)} %fusion.34), kind=kLoop, calls=%fused_computation.54 | loop fusion | flops 18348288 | bytes 14956544 | tf_op jit(solution)/shard_map/reduce_sum | solution.py:97
  75.9 7.6 %fusion.48 = f32[128,2,7]{0,2,1:T(8,128)S(1)} fusion(bf16[2048,2,128,1]{0,2,3,1:T(8,128)(2,1)S(1)} %bitcast.165, f32[2,128,7,2048]{3,1,2,0:T(8,128)} %copy-done, f32[128,2,7]{0,2,1:T(8,128)S(1)} %broadcast_maximum_fusion, pred[128,2048]{1,0:T(8,128)(4,1)S(1)} %fusion.34, bf16[128,2,7,128]{0,3,2,1:T(8,128)(2,1)S(1)} %broadcast_select_fusion, ...), kind=kOutput, calls=%fused_computation.68 | convolution fusion | flops 959248640 | bytes 16471040 | tf_op jit(solution)/shard_map/qhgk,khd->qhgd/dot_general | solution.py:98
  83.5 218.9 %while.23 = (s32[]{:T(128)}, bf16[128,512]{0,1:T(8,128)(2,1)S(1)}, f32[128,512]{0,1:T(8,128)S(1)}, f32[128,2,7,128]{3,0,2,1:T(8,128)S(1)}, s32[]{:T(128)}, /*ind...) while((s32[]{:T(128)}, bf16[128,512]{0,1:T(8,128)(2,1)S(1)}, ...), condition=%wide.region_4.5_spmd.clone.clone.clone, body=%wide.region_3.4_spmd.clone.clone.clone.sunk | while | flops 296830464 | bytes 10938793 | solution.py:155
  83.5 2.7 collective-permute-start
  87.0 1.3 fusion.117
  89.8 2.2 collective-permute-start.1
  92.5 1.5 collective-permute-done.1
  94.0 4.4 %collective-permute-start = (bf16[128,512]{0,1:T(8,128)(2,1)S(1)}, bf16[128,512]{0,1:T(8,128)(2,1)S(1)}, u32[]{:S(2)}, u32[]{:S(2)}) collective-permute-start(bf16[128,512]{0,1:T(8,128)(2,1)S(1)} %copy.63), channel_id=1, source_target_pairs={{0,32},{32,64},{64,96},{96,128},{128,160},{160,192},{192,224},{224... | collective-permute-start | bytes 393224 | tf_op jit(solution)/shard_map/while/body/eval_jaxpr/ppermute | solution.py:17
  99.1 1.3 fusion.117
  102.0 1.9 collective-permute-start.1
  104.4 2.0 collective-permute-done.1
  106.4 3.9 collective-permute-start
  111.0 1.3 fusion.117
  113.9 1.9 collective-permute-start.1
  116.2 4.1 collective-permute-done.1
  120.4 1.9 collective-permute-start
  123.0 1.3 fusion.117
  125.9 1.9 collective-permute-start.1
  128.3 6.0 %collective-permute-done.1 = bf16[128,512]{0,1:T(8,128)(2,1)S(1)} collective-permute-done((bf16[128,512]{0,1:T(8,128)(2,1)S(1)}, bf16[128,512]{0,1:T(8,128)(2,1)S(1)}, u32[]{:S(2)}, u32[]{:S(2)}) %collective-permute-start.1) | collective-permute-done | bytes 131104 | tf_op jit(solution)/shard_map/while/body/eval_jaxpr/ppermute | solution.py:17
  134.4 1.9 collective-permute-start
  139.9 1.9 collective-permute-start.1
  142.3 6.0 %collective-permute-done.1 = bf16[128,512]{0,1:T(8,128)(2,1)S(1)} collective-permute-done((bf16[128,512]{0,1:T(8,128)(2,1)S(1)}, bf16[128,512]{0,1:T(8,128)(2,1)S(1)}, u32[]{:S(2)}, u32[]{:S(2)}) %collective-permute-start.1) | collective-permute-done | bytes 131104 | tf_op jit(solution)/shard_map/while/body/eval_jaxpr/ppermute | solution.py:17
  148.4 1.9 collective-permute-start
  153.9 1.9 collective-permute-start.1
  156.3 6.0 %collective-permute-done.1 = bf16[128,512]{0,1:T(8,128)(2,1)S(1)} collective-permute-done((bf16[128,512]{0,1:T(8,128)(2,1)S(1)}, bf16[128,512]{0,1:T(8,128)(2,1)S(1)}, u32[]{:S(2)}, u32[]{:S(2)}) %collective-permute-start.1) | collective-permute-done | bytes 131104 | tf_op jit(solution)/shard_map/while/body/eval_jaxpr/ppermute | solution.py:17
  162.4 1.9 collective-permute-start
  167.9 1.9 collective-permute-start.1
  170.3 6.0 %collective-permute-done.1 = bf16[128,512]{0,1:T(8,128)(2,1)S(1)} collective-permute-done((bf16[128,512]{0,1:T(8,128)(2,1)S(1)}, bf16[128,512]{0,1:T(8,128)(2,1)S(1)}, u32[]{:S(2)}, u32[]{:S(2)}) %collective-permute-start.1) | collective-permute-done | bytes 131104 | tf_op jit(solution)/shard_map/while/body/eval_jaxpr/ppermute | solution.py:17
  176.4 1.9 collective-permute-start
  181.9 1.9 collective-permute-start.1
  184.3 6.0 %collective-permute-done.1 = bf16[128,512]{0,1:T(8,128)(2,1)S(1)} collective-permute-done((bf16[128,512]{0,1:T(8,128)(2,1)S(1)}, bf16[128,512]{0,1:T(8,128)(2,1)S(1)}, u32[]{:S(2)}, u32[]{:S(2)}) %collective-permute-start.1) | collective-permute-done | bytes 131104 | tf_op jit(solution)/shard_map/while/body/eval_jaxpr/ppermute | solution.py:17
  190.4 1.9 collective-permute-start
  195.9 1.9 collective-permute-start.1
  198.3 6.0 %collective-permute-done.1 = bf16[128,512]{0,1:T(8,128)(2,1)S(1)} collective-permute-done((bf16[128,512]{0,1:T(8,128)(2,1)S(1)}, bf16[128,512]{0,1:T(8,128)(2,1)S(1)}, u32[]{:S(2)}, u32[]{:S(2)}) %collective-permute-start.1) | collective-permute-done | bytes 131104 | tf_op jit(solution)/shard_map/while/body/eval_jaxpr/ppermute | solution.py:17
  204.4 1.9 collective-permute-start
  210.0 1.9 collective-permute-start.1
  212.3 6.0 %collective-permute-done.1 = bf16[128,512]{0,1:T(8,128)(2,1)S(1)} collective-permute-done((bf16[128,512]{0,1:T(8,128)(2,1)S(1)}, bf16[128,512]{0,1:T(8,128)(2,1)S(1)}, u32[]{:S(2)}, u32[]{:S(2)}) %collective-permute-start.1) | collective-permute-done | bytes 131104 | tf_op jit(solution)/shard_map/while/body/eval_jaxpr/ppermute | solution.py:17
  218.4 1.9 collective-permute-start
  224.0 1.9 collective-permute-start.1
  226.3 6.0 %collective-permute-done.1 = bf16[128,512]{0,1:T(8,128)(2,1)S(1)} collective-permute-done((bf16[128,512]{0,1:T(8,128)(2,1)S(1)}, bf16[128,512]{0,1:T(8,128)(2,1)S(1)}, u32[]{:S(2)}, u32[]{:S(2)}) %collective-permute-start.1) | collective-permute-done | bytes 131104 | tf_op jit(solution)/shard_map/while/body/eval_jaxpr/ppermute | solution.py:17
  232.4 1.9 collective-permute-start
  238.0 1.9 collective-permute-start.1
  240.3 6.0 %collective-permute-done.1 = bf16[128,512]{0,1:T(8,128)(2,1)S(1)} collective-permute-done((bf16[128,512]{0,1:T(8,128)(2,1)S(1)}, bf16[128,512]{0,1:T(8,128)(2,1)S(1)}, u32[]{:S(2)}, u32[]{:S(2)}) %collective-permute-start.1) | collective-permute-done | bytes 131104 | tf_op jit(solution)/shard_map/while/body/eval_jaxpr/ppermute | solution.py:17
  246.4 1.9 collective-permute-start
  249.1 1.3 fusion.117
  252.0 1.9 collective-permute-start.1
  254.3 6.0 %collective-permute-done.1 = bf16[128,512]{0,1:T(8,128)(2,1)S(1)} collective-permute-done((bf16[128,512]{0,1:T(8,128)(2,1)S(1)}, bf16[128,512]{0,1:T(8,128)(2,1)S(1)}, u32[]{:S(2)}, u32[]{:S(2)}) %collective-permute-start.1) | collective-permute-done | bytes 131104 | tf_op jit(solution)/shard_map/while/body/eval_jaxpr/ppermute | solution.py:17
  260.4 1.9 collective-permute-start
  266.0 1.9 collective-permute-start.1
  268.3 6.0 %collective-permute-done.1 = bf16[128,512]{0,1:T(8,128)(2,1)S(1)} collective-permute-done((bf16[128,512]{0,1:T(8,128)(2,1)S(1)}, bf16[128,512]{0,1:T(8,128)(2,1)S(1)}, u32[]{:S(2)}, u32[]{:S(2)}) %collective-permute-start.1) | collective-permute-done | bytes 131104 | tf_op jit(solution)/shard_map/while/body/eval_jaxpr/ppermute | solution.py:17
  274.4 1.9 collective-permute-start
  277.1 1.3 fusion.117
  280.0 1.9 collective-permute-start.1
  282.4 6.0 %collective-permute-done.1 = bf16[128,512]{0,1:T(8,128)(2,1)S(1)} collective-permute-done((bf16[128,512]{0,1:T(8,128)(2,1)S(1)}, bf16[128,512]{0,1:T(8,128)(2,1)S(1)}, u32[]{:S(2)}, u32[]{:S(2)}) %collective-permute-start.1) | collective-permute-done | bytes 131104 | tf_op jit(solution)/shard_map/while/body/eval_jaxpr/ppermute | solution.py:17
  288.4 1.9 collective-permute-start
  294.0 1.9 collective-permute-start.1
  296.4 6.0 %collective-permute-done.1 = bf16[128,512]{0,1:T(8,128)(2,1)S(1)} collective-permute-done((bf16[128,512]{0,1:T(8,128)(2,1)S(1)}, bf16[128,512]{0,1:T(8,128)(2,1)S(1)}, u32[]{:S(2)}, u32[]{:S(2)}) %collective-permute-start.1) | collective-permute-done | bytes 131104 | tf_op jit(solution)/shard_map/while/body/eval_jaxpr/ppermute | solution.py:17
  305.0 108.8 %all-reduce = (f32[1792]{0:T(1024)}, f32[256]{0:T(256)}) all-reduce(f32[1792]{0:T(1024)S(1)} %reduce_sum.41, f32[256]{0:T(256)S(1)} %slice_reduce_fusion), channel_id=1, replica_groups=mesh['seq'=16,'pair'=32] {'seq','pair'}, use_global_device_ids=true, to_apply=%region_6.7 | all-reduce | flops 2048 | bytes 16384 | tf_op jit(solution)/shard_map/psum | solution.py:159
  (293 shorter events, 65.4 us)
Async XLA Ops:
  7.2 54.3 %all-gather.3.cloned.1.call-start = ((), (), s32[]{:S(2)}) async-start(), calls=%async_computation | async-start | bytes 2228224 | tf_op jit(solution)/shard_map/all_gather | solution.py:91
  66.0 5.2 %copy-start = (f32[2,128,7,2048]{3,1,2,0:T(8,128)}, f32[2,128,7,2048]{3,1,2,0:T(8,128)S(1)}, u32[]{:S(2)}) copy-start(f32[2,128,7,2048]{3,1,2,0:T(8,128)S(1)} %get-tuple-element.517) | copy-start | bytes 44040196
  75.9 7.6 %copy-start.1 = (bf16[1,128,512]{1,2,0:T(8,128)(2,1)S(1)}, bf16[1,128,512]{1,2,0:T(8,128)(2,1)}, u32[]{:S(2)}) copy-start(bf16[1,128,512]{1,2,0:T(8,128)(2,1)} %copy.28) | copy-start | bytes 393220
  75.9 7.6 %copy-start.2 = (s32[1,2]{1,0:T(1,128)S(1)}, s32[1,2]{1,0:T(1,128)}, u32[]{:S(2)}) copy-start(s32[1,2]{1,0:T(1,128)} %param.10) | copy-start | bytes 28
  83.5 10.4 %collective-permute-start = (bf16[128,512]{0,1:T(8,128)(2,1)S(1)}, bf16[128,512]{0,1:T(8,128)(2,1)S(1)}, u32[]{:S(2)}, u32[]{:S(2)}) collective-permute-start(bf16[128,512]{0,1:T(8,128)(2,1)S(1)} %copy.63), channel_id=1, source_target_pairs={{0,32},{32,64},{64,96},{96,128},{128,160},{160,192},{192,224},{224... | collective-permute-start | bytes 393224 | tf_op jit(solution)/shard_map/while/body/eval_jaxpr/ppermute | solution.py:17
  89.8 4.1 collective-permute-start.1
  94.0 12.3 %collective-permute-start = (bf16[128,512]{0,1:T(8,128)(2,1)S(1)}, bf16[128,512]{0,1:T(8,128)(2,1)S(1)}, u32[]{:S(2)}, u32[]{:S(2)}) collective-permute-start(bf16[128,512]{0,1:T(8,128)(2,1)S(1)} %copy.63), channel_id=1, source_target_pairs={{0,32},{32,64},{64,96},{96,128},{128,160},{160,192},{192,224},{224... | collective-permute-start | bytes 393224 | tf_op jit(solution)/shard_map/while/body/eval_jaxpr/ppermute | solution.py:17
  102.0 4.3 %collective-permute-start.1 = (bf16[128,512]{0,1:T(8,128)(2,1)S(1)}, bf16[128,512]{0,1:T(8,128)(2,1)S(1)}, u32[]{:S(2)}, u32[]{:S(2)}) collective-permute-start(bf16[128,512]{0,1:T(8,128)(2,1)S(1)} %fusion.123), channel_id=1, source_target_pairs={{0,32},{32,64},{64,96},{96,128},{128,160},{160,192},{192,224},{224... | collective-permute-start | bytes 393224 | tf_op jit(solution)/shard_map/while/body/eval_jaxpr/ppermute | solution.py:17
  106.4 14.0 %collective-permute-start = (bf16[128,512]{0,1:T(8,128)(2,1)S(1)}, bf16[128,512]{0,1:T(8,128)(2,1)S(1)}, u32[]{:S(2)}, u32[]{:S(2)}) collective-permute-start(bf16[128,512]{0,1:T(8,128)(2,1)S(1)} %copy.63), channel_id=1, source_target_pairs={{0,32},{32,64},{64,96},{96,128},{128,160},{160,192},{192,224},{224... | collective-permute-start | bytes 393224 | tf_op jit(solution)/shard_map/while/body/eval_jaxpr/ppermute | solution.py:17
  113.9 6.5 %collective-permute-start.1 = (bf16[128,512]{0,1:T(8,128)(2,1)S(1)}, bf16[128,512]{0,1:T(8,128)(2,1)S(1)}, u32[]{:S(2)}, u32[]{:S(2)}) collective-permute-start(bf16[128,512]{0,1:T(8,128)(2,1)S(1)} %fusion.123), channel_id=1, source_target_pairs={{0,32},{32,64},{64,96},{96,128},{128,160},{160,192},{192,224},{224... | collective-permute-start | bytes 393224 | tf_op jit(solution)/shard_map/while/body/eval_jaxpr/ppermute | solution.py:17
  120.4 14.0 %collective-permute-start = (bf16[128,512]{0,1:T(8,128)(2,1)S(1)}, bf16[128,512]{0,1:T(8,128)(2,1)S(1)}, u32[]{:S(2)}, u32[]{:S(2)}) collective-permute-start(bf16[128,512]{0,1:T(8,128)(2,1)S(1)} %copy.63), channel_id=1, source_target_pairs={{0,32},{32,64},{64,96},{96,128},{128,160},{160,192},{192,224},{224... | collective-permute-start | bytes 393224 | tf_op jit(solution)/shard_map/while/body/eval_jaxpr/ppermute | solution.py:17
  125.9 8.4 %collective-permute-start.1 = (bf16[128,512]{0,1:T(8,128)(2,1)S(1)}, bf16[128,512]{0,1:T(8,128)(2,1)S(1)}, u32[]{:S(2)}, u32[]{:S(2)}) collective-permute-start(bf16[128,512]{0,1:T(8,128)(2,1)S(1)} %fusion.123), channel_id=1, source_target_pairs={{0,32},{32,64},{64,96},{96,128},{128,160},{160,192},{192,224},{224... | collective-permute-start | bytes 393224 | tf_op jit(solution)/shard_map/while/body/eval_jaxpr/ppermute | solution.py:17
  134.4 14.0 %collective-permute-start = (bf16[128,512]{0,1:T(8,128)(2,1)S(1)}, bf16[128,512]{0,1:T(8,128)(2,1)S(1)}, u32[]{:S(2)}, u32[]{:S(2)}) collective-permute-start(bf16[128,512]{0,1:T(8,128)(2,1)S(1)} %copy.63), channel_id=1, source_target_pairs={{0,32},{32,64},{64,96},{96,128},{128,160},{160,192},{192,224},{224... | collective-permute-start | bytes 393224 | tf_op jit(solution)/shard_map/while/body/eval_jaxpr/ppermute | solution.py:17
  139.9 8.4 %collective-permute-start.1 = (bf16[128,512]{0,1:T(8,128)(2,1)S(1)}, bf16[128,512]{0,1:T(8,128)(2,1)S(1)}, u32[]{:S(2)}, u32[]{:S(2)}) collective-permute-start(bf16[128,512]{0,1:T(8,128)(2,1)S(1)} %fusion.123), channel_id=1, source_target_pairs={{0,32},{32,64},{64,96},{96,128},{128,160},{160,192},{192,224},{224... | collective-permute-start | bytes 393224 | tf_op jit(solution)/shard_map/while/body/eval_jaxpr/ppermute | solution.py:17
  148.4 14.0 %collective-permute-start = (bf16[128,512]{0,1:T(8,128)(2,1)S(1)}, bf16[128,512]{0,1:T(8,128)(2,1)S(1)}, u32[]{:S(2)}, u32[]{:S(2)}) collective-permute-start(bf16[128,512]{0,1:T(8,128)(2,1)S(1)} %copy.63), channel_id=1, source_target_pairs={{0,32},{32,64},{64,96},{96,128},{128,160},{160,192},{192,224},{224... | collective-permute-start | bytes 393224 | tf_op jit(solution)/shard_map/while/body/eval_jaxpr/ppermute | solution.py:17
  153.9 8.4 %collective-permute-start.1 = (bf16[128,512]{0,1:T(8,128)(2,1)S(1)}, bf16[128,512]{0,1:T(8,128)(2,1)S(1)}, u32[]{:S(2)}, u32[]{:S(2)}) collective-permute-start(bf16[128,512]{0,1:T(8,128)(2,1)S(1)} %fusion.123), channel_id=1, source_target_pairs={{0,32},{32,64},{64,96},{96,128},{128,160},{160,192},{192,224},{224... | collective-permute-start | bytes 393224 | tf_op jit(solution)/shard_map/while/body/eval_jaxpr/ppermute | solution.py:17
  162.4 14.0 %collective-permute-start = (bf16[128,512]{0,1:T(8,128)(2,1)S(1)}, bf16[128,512]{0,1:T(8,128)(2,1)S(1)}, u32[]{:S(2)}, u32[]{:S(2)}) collective-permute-start(bf16[128,512]{0,1:T(8,128)(2,1)S(1)} %copy.63), channel_id=1, source_target_pairs={{0,32},{32,64},{64,96},{96,128},{128,160},{160,192},{192,224},{224... | collective-permute-start | bytes 393224 | tf_op jit(solution)/shard_map/while/body/eval_jaxpr/ppermute | solution.py:17
  167.9 8.4 %collective-permute-start.1 = (bf16[128,512]{0,1:T(8,128)(2,1)S(1)}, bf16[128,512]{0,1:T(8,128)(2,1)S(1)}, u32[]{:S(2)}, u32[]{:S(2)}) collective-permute-start(bf16[128,512]{0,1:T(8,128)(2,1)S(1)} %fusion.123), channel_id=1, source_target_pairs={{0,32},{32,64},{64,96},{96,128},{128,160},{160,192},{192,224},{224... | collective-permute-start | bytes 393224 | tf_op jit(solution)/shard_map/while/body/eval_jaxpr/ppermute | solution.py:17
  176.4 14.0 %collective-permute-start = (bf16[128,512]{0,1:T(8,128)(2,1)S(1)}, bf16[128,512]{0,1:T(8,128)(2,1)S(1)}, u32[]{:S(2)}, u32[]{:S(2)}) collective-permute-start(bf16[128,512]{0,1:T(8,128)(2,1)S(1)} %copy.63), channel_id=1, source_target_pairs={{0,32},{32,64},{64,96},{96,128},{128,160},{160,192},{192,224},{224... | collective-permute-start | bytes 393224 | tf_op jit(solution)/shard_map/while/body/eval_jaxpr/ppermute | solution.py:17
  181.9 8.4 %collective-permute-start.1 = (bf16[128,512]{0,1:T(8,128)(2,1)S(1)}, bf16[128,512]{0,1:T(8,128)(2,1)S(1)}, u32[]{:S(2)}, u32[]{:S(2)}) collective-permute-start(bf16[128,512]{0,1:T(8,128)(2,1)S(1)} %fusion.123), channel_id=1, source_target_pairs={{0,32},{32,64},{64,96},{96,128},{128,160},{160,192},{192,224},{224... | collective-permute-start | bytes 393224 | tf_op jit(solution)/shard_map/while/body/eval_jaxpr/ppermute | solution.py:17
  190.4 14.0 %collective-permute-start = (bf16[128,512]{0,1:T(8,128)(2,1)S(1)}, bf16[128,512]{0,1:T(8,128)(2,1)S(1)}, u32[]{:S(2)}, u32[]{:S(2)}) collective-permute-start(bf16[128,512]{0,1:T(8,128)(2,1)S(1)} %copy.63), channel_id=1, source_target_pairs={{0,32},{32,64},{64,96},{96,128},{128,160},{160,192},{192,224},{224... | collective-permute-start | bytes 393224 | tf_op jit(solution)/shard_map/while/body/eval_jaxpr/ppermute | solution.py:17
  195.9 8.4 %collective-permute-start.1 = (bf16[128,512]{0,1:T(8,128)(2,1)S(1)}, bf16[128,512]{0,1:T(8,128)(2,1)S(1)}, u32[]{:S(2)}, u32[]{:S(2)}) collective-permute-start(bf16[128,512]{0,1:T(8,128)(2,1)S(1)} %fusion.123), channel_id=1, source_target_pairs={{0,32},{32,64},{64,96},{96,128},{128,160},{160,192},{192,224},{224... | collective-permute-start | bytes 393224 | tf_op jit(solution)/shard_map/while/body/eval_jaxpr/ppermute | solution.py:17
  204.4 14.0 %collective-permute-start = (bf16[128,512]{0,1:T(8,128)(2,1)S(1)}, bf16[128,512]{0,1:T(8,128)(2,1)S(1)}, u32[]{:S(2)}, u32[]{:S(2)}) collective-permute-start(bf16[128,512]{0,1:T(8,128)(2,1)S(1)} %copy.63), channel_id=1, source_target_pairs={{0,32},{32,64},{64,96},{96,128},{128,160},{160,192},{192,224},{224... | collective-permute-start | bytes 393224 | tf_op jit(solution)/shard_map/while/body/eval_jaxpr/ppermute | solution.py:17
  210.0 8.4 %collective-permute-start.1 = (bf16[128,512]{0,1:T(8,128)(2,1)S(1)}, bf16[128,512]{0,1:T(8,128)(2,1)S(1)}, u32[]{:S(2)}, u32[]{:S(2)}) collective-permute-start(bf16[128,512]{0,1:T(8,128)(2,1)S(1)} %fusion.123), channel_id=1, source_target_pairs={{0,32},{32,64},{64,96},{96,128},{128,160},{160,192},{192,224},{224... | collective-permute-start | bytes 393224 | tf_op jit(solution)/shard_map/while/body/eval_jaxpr/ppermute | solution.py:17
  218.4 14.0 %collective-permute-start = (bf16[128,512]{0,1:T(8,128)(2,1)S(1)}, bf16[128,512]{0,1:T(8,128)(2,1)S(1)}, u32[]{:S(2)}, u32[]{:S(2)}) collective-permute-start(bf16[128,512]{0,1:T(8,128)(2,1)S(1)} %copy.63), channel_id=1, source_target_pairs={{0,32},{32,64},{64,96},{96,128},{128,160},{160,192},{192,224},{224... | collective-permute-start | bytes 393224 | tf_op jit(solution)/shard_map/while/body/eval_jaxpr/ppermute | solution.py:17
  224.0 8.4 %collective-permute-start.1 = (bf16[128,512]{0,1:T(8,128)(2,1)S(1)}, bf16[128,512]{0,1:T(8,128)(2,1)S(1)}, u32[]{:S(2)}, u32[]{:S(2)}) collective-permute-start(bf16[128,512]{0,1:T(8,128)(2,1)S(1)} %fusion.123), channel_id=1, source_target_pairs={{0,32},{32,64},{64,96},{96,128},{128,160},{160,192},{192,224},{224... | collective-permute-start | bytes 393224 | tf_op jit(solution)/shard_map/while/body/eval_jaxpr/ppermute | solution.py:17
  232.4 14.0 %collective-permute-start = (bf16[128,512]{0,1:T(8,128)(2,1)S(1)}, bf16[128,512]{0,1:T(8,128)(2,1)S(1)}, u32[]{:S(2)}, u32[]{:S(2)}) collective-permute-start(bf16[128,512]{0,1:T(8,128)(2,1)S(1)} %copy.63), channel_id=1, source_target_pairs={{0,32},{32,64},{64,96},{96,128},{128,160},{160,192},{192,224},{224... | collective-permute-start | bytes 393224 | tf_op jit(solution)/shard_map/while/body/eval_jaxpr/ppermute | solution.py:17
  238.0 8.4 %collective-permute-start.1 = (bf16[128,512]{0,1:T(8,128)(2,1)S(1)}, bf16[128,512]{0,1:T(8,128)(2,1)S(1)}, u32[]{:S(2)}, u32[]{:S(2)}) collective-permute-start(bf16[128,512]{0,1:T(8,128)(2,1)S(1)} %fusion.123), channel_id=1, source_target_pairs={{0,32},{32,64},{64,96},{96,128},{128,160},{160,192},{192,224},{224... | collective-permute-start | bytes 393224 | tf_op jit(solution)/shard_map/while/body/eval_jaxpr/ppermute | solution.py:17
  246.4 14.0 %collective-permute-start = (bf16[128,512]{0,1:T(8,128)(2,1)S(1)}, bf16[128,512]{0,1:T(8,128)(2,1)S(1)}, u32[]{:S(2)}, u32[]{:S(2)}) collective-permute-start(bf16[128,512]{0,1:T(8,128)(2,1)S(1)} %copy.63), channel_id=1, source_target_pairs={{0,32},{32,64},{64,96},{96,128},{128,160},{160,192},{192,224},{224... | collective-permute-start | bytes 393224 | tf_op jit(solution)/shard_map/while/body/eval_jaxpr/ppermute | solution.py:17
  252.0 8.4 %collective-permute-start.1 = (bf16[128,512]{0,1:T(8,128)(2,1)S(1)}, bf16[128,512]{0,1:T(8,128)(2,1)S(1)}, u32[]{:S(2)}, u32[]{:S(2)}) collective-permute-start(bf16[128,512]{0,1:T(8,128)(2,1)S(1)} %fusion.123), channel_id=1, source_target_pairs={{0,32},{32,64},{64,96},{96,128},{128,160},{160,192},{192,224},{224... | collective-permute-start | bytes 393224 | tf_op jit(solution)/shard_map/while/body/eval_jaxpr/ppermute | solution.py:17
  260.4 14.0 %collective-permute-start = (bf16[128,512]{0,1:T(8,128)(2,1)S(1)}, bf16[128,512]{0,1:T(8,128)(2,1)S(1)}, u32[]{:S(2)}, u32[]{:S(2)}) collective-permute-start(bf16[128,512]{0,1:T(8,128)(2,1)S(1)} %copy.63), channel_id=1, source_target_pairs={{0,32},{32,64},{64,96},{96,128},{128,160},{160,192},{192,224},{224... | collective-permute-start | bytes 393224 | tf_op jit(solution)/shard_map/while/body/eval_jaxpr/ppermute | solution.py:17
  266.0 8.4 %collective-permute-start.1 = (bf16[128,512]{0,1:T(8,128)(2,1)S(1)}, bf16[128,512]{0,1:T(8,128)(2,1)S(1)}, u32[]{:S(2)}, u32[]{:S(2)}) collective-permute-start(bf16[128,512]{0,1:T(8,128)(2,1)S(1)} %fusion.123), channel_id=1, source_target_pairs={{0,32},{32,64},{64,96},{96,128},{128,160},{160,192},{192,224},{224... | collective-permute-start | bytes 393224 | tf_op jit(solution)/shard_map/while/body/eval_jaxpr/ppermute | solution.py:17
  274.4 14.0 %collective-permute-start = (bf16[128,512]{0,1:T(8,128)(2,1)S(1)}, bf16[128,512]{0,1:T(8,128)(2,1)S(1)}, u32[]{:S(2)}, u32[]{:S(2)}) collective-permute-start(bf16[128,512]{0,1:T(8,128)(2,1)S(1)} %copy.63), channel_id=1, source_target_pairs={{0,32},{32,64},{64,96},{96,128},{128,160},{160,192},{192,224},{224... | collective-permute-start | bytes 393224 | tf_op jit(solution)/shard_map/while/body/eval_jaxpr/ppermute | solution.py:17
  280.0 8.4 %collective-permute-start.1 = (bf16[128,512]{0,1:T(8,128)(2,1)S(1)}, bf16[128,512]{0,1:T(8,128)(2,1)S(1)}, u32[]{:S(2)}, u32[]{:S(2)}) collective-permute-start(bf16[128,512]{0,1:T(8,128)(2,1)S(1)} %fusion.123), channel_id=1, source_target_pairs={{0,32},{32,64},{64,96},{96,128},{128,160},{160,192},{192,224},{224... | collective-permute-start | bytes 393224 | tf_op jit(solution)/shard_map/while/body/eval_jaxpr/ppermute | solution.py:17
  288.4 14.0 %collective-permute-start = (bf16[128,512]{0,1:T(8,128)(2,1)S(1)}, bf16[128,512]{0,1:T(8,128)(2,1)S(1)}, u32[]{:S(2)}, u32[]{:S(2)}) collective-permute-start(bf16[128,512]{0,1:T(8,128)(2,1)S(1)} %copy.63), channel_id=1, source_target_pairs={{0,32},{32,64},{64,96},{96,128},{128,160},{160,192},{192,224},{224... | collective-permute-start | bytes 393224 | tf_op jit(solution)/shard_map/while/body/eval_jaxpr/ppermute | solution.py:17
  294.0 8.4 %collective-permute-start.1 = (bf16[128,512]{0,1:T(8,128)(2,1)S(1)}, bf16[128,512]{0,1:T(8,128)(2,1)S(1)}, u32[]{:S(2)}, u32[]{:S(2)}) collective-permute-start(bf16[128,512]{0,1:T(8,128)(2,1)S(1)} %fusion.123), channel_id=1, source_target_pairs={{0,32},{32,64},{64,96},{96,128},{128,160},{160,192},{192,224},{224... | collective-permute-start | bytes 393224 | tf_op jit(solution)/shard_map/while/body/eval_jaxpr/ppermute | solution.py:17
Sparse Core Ops, SparseCore 0:
  10.6 50.8 all-gather.2
where the time goes:
time: 422 us; the launch traced here: 421 us
  waiting for transfers between devices  130 us (31%)
  blocking collectives  109 us (26%)
  starting transfers between devices  66.9 us (16%)
  matrix products  39.5 us (9%)
  other arithmetic  33.2 us (8%)
  local copies, waits for them, and re-layouts  25.3 us (6%)
  between operations  14.2 us (3%)
    psum x1, blocking collectives, on_device(): lax.psum((grad_q.sum(0), grads[:, KEY_VALUE_HEADS * HEAD_SIZE:].sum(0)),...  109 us
    ppermute x32, waiting for transfers between devices, passed_along(): lax.ppermute(shard, axis, [(i, (i + by) % count) for i in range(count)])  85.8 us
    ppermute x32, starting transfers between devices, passed_along(): lax.ppermute(shard, axis, [(i, (i + by) % count) for i in range(count)])  66.9 us
    all_gather x1, waiting for transfers between devices, on_device(): piece = lax.all_gather(kv_local, 'seq', axis=0, tiled=True)  44.6 us
    lt x17, other arithmetic, visible(): k_place < k_limit  21.7 us
    slice x17, local copies, waits for them, and re-layouts, visible(): k_limit = jnp.where(k_kind == 1, lengths[0], lengths[1])  10.8 us
    dot_general x17, matrix products, block_scores(): jnp.einsum('qhgd,khd->qhgk', query_head_rows, key_rows, preferred_element...  9.84 us
    unnamed x9, local copies, waits for them, and re-layouts  9.37 us
  transfers between devices with their start and end apart: 33, of which 17 were waited for; matrix products, arithmetic and copies ran while one was open for 17% of the time, Pallas kernels for 0%

commit v1 on v0

v1 whole, which is shorter than its diff:
```python
import functools
import math

import jax
import jax.numpy as jnp
from jax import lax
from jax.experimental import pallas as pl
from jax.experimental.pallas import tpu as pltpu
from jax.sharding import PartitionSpec as P

HEADS = 7
DIM = 128
ROWS = 128
LANES = HEADS * 2 * ROWS
RLANES = HEADS * ROWS
UNITS = 4
SCALE = 1.0 / math.sqrt(DIM)
C2 = SCALE * math.log2(math.e)
NEG = -1e30
MESH = pl.DeviceIdType.MESH
F32, BF16 = jnp.float32, jnp.bfloat16


def xor(value, mask):
    out = value
    bit = 1
    while bit <= mask:
        if mask & bit:
            out = out + bit - 2 * bit * ((value // bit) % 2)
        bit *= 2
    return out


def dot_nt(a, b):
    return lax.dot_general(a, b, (((1,), (1,)), ((), ())), preferred_element_type=F32)


def dot(a, b):
    return jnp.dot(a, b, preferred_element_type=F32)


def kernel(
    pair_near,
    pair_far,
    q_hbm,
    kv_hbm,
    cot_hbm,
    len_ref,
    bias_ref,
    dq_hbm,
    dkv_ref,
    bq_ref,
    bv_ref,
    kvs,
    kvg,
    qin,
    doin,
    qcat,
    docat,
    bq3,
    bdo3,
    kp,
    vp,
    k3,
    v3,
    kt,
    kt3,
    bias12,
    bias3,
    prob,
    gprob,
    prob3,
    gprob3,
    st,
    st3,
    wrow,
    pb,
    dsb,
    p3b,
    ds3b,
    stage,
    rs,
    dqst,
    vec,
    ar1,
    ar2,
    ar3,
    ar4,
    loc_sem,
    kv_send,
    kv_recv,
    x_send,
    x_recv,
    rs_send,
    rs_recv,
    dq_sem,
    a_send,
    a_recv,
):
    s = lax.axis_index("seq")
    p = lax.axis_index("pair")
    chip = s // 2
    core = s % 2
    other = 1 - core
    duo = s // 4
    near, far = pair_near, pair_far

    def seq_dev(m):
        return {"seq": xor(s, m), "pair": p}

    def pair_dev(n):
        return {"seq": s, "pair": xor(p, n)}

    own_cols = pl.ds(pl.multiple_of(core * RLANES, 128), RLANES)
    other_cols = pl.ds(pl.multiple_of(other * RLANES, 128), RLANES)

    local = []
    for h in range(2):
        for part in range(2):
            local.append(
                pltpu.make_async_copy(
                    kv_hbm.at[:, pl.ds((2 * part + h) * DIM, DIM)],
                    kvs.at[h, part],
                    loc_sem.at[2 * h + part],
                )
            )
    local.append(pltpu.make_async_copy(q_hbm.at[:, own_cols], qin.at[core], loc_sem.at[4]))
    local.append(pltpu.make_async_copy(cot_hbm.at[:, own_cols], doin.at[core], loc_sem.at[5]))
    for cp in local:
        cp.start()

    barrier = pltpu.get_barrier_semaphore()
    for m in range(1, 16):
        pl.semaphore_signal(barrier, inc=1, device_id=seq_dev(m), device_id_type=MESH)
    for n in near + far:
        pl.semaphore_signal(barrier, inc=1, device_id=pair_dev(n), device_id_type=MESH)
    for cp in local[:4]:
        cp.wait()
    pl.semaphore_wait(barrier, 15 + len(near) + len(far))

    def remote(src, dst, send, recv, dev):
        return pltpu.make_async_remote_copy(
            src_ref=src,
            dst_ref=dst,
            send_sem=send,
            recv_sem=recv,
            device_id=dev,
            device_id_type=MESH,
        )

    qx = remote(q_hbm.at[:, other_cols], qin.at[core], x_send.at[0], x_recv.at[0], seq_dev(1))
    dx = remote(cot_hbm.at[:, other_cols], doin.at[core], x_send.at[1], x_recv.at[1], seq_dev(1))
    qx.start()
    dx.start()
    pushes = []
    for m in range(1, 16):
        head = xor(s, m) % 2
        cp = remote(kvs.at[head], kvg.at[s], kv_send.at[m], kv_recv.at[m], seq_dev(m))
        cp.start()
        pushes.append(cp)
    kvg[s] = kvs[core]

    len0, len1 = len_ref[0, 0], len_ref[0, 1]
    key = lax.broadcasted_iota(jnp.int32, (256, 128), 0)
    lane = lax.broadcasted_iota(jnp.int32, (256, 128), 1)
    bias12[...] = jnp.where(key + 256 * duo <= lane + 128 * chip, 0.0, NEG).astype(F32)
    key = lax.broadcasted_iota(jnp.int32, (128, 128), 0)
    lane = lax.broadcasted_iota(jnp.int32, (128, 128), 1)
    place_q = jnp.where(lane < 64, lane, lane - 64) + 64 * chip
    limit = jnp.where(lane < 64, len0, len1)
    for u in range(UNITS):
        place_k = key + 128 * xor(duo, u)
        seen = (place_k <= place_q) & (place_k < limit)
        bias3[u] = jnp.where(seen, 0.0, NEG).astype(F32)

    bq3[...] = jnp.zeros_like(bq3)
    bdo3[...] = jnp.zeros_like(bdo3)
    row = lax.broadcasted_iota(jnp.int32, (32, 128), 0)

    def prepare(blk):
        base = 32 * (2 * chip + blk)
        for h in range(HEADS):
            cols = pl.ds(h * DIM, DIM)
            bias = bias_ref[:, pl.ds(pl.multiple_of((core * HEADS + h) * DIM, 128), DIM)]
            x = (qin[blk, :, cols].astype(F32) + bias).astype(BF16)
            d = doin[blk, :, cols]
            d1 = jnp.where(row + base < len0, d[64:96].astype(F32), 0.0).astype(BF16)
            d2 = jnp.where(row + base < len1, d[96:128].astype(F32), 0.0).astype(BF16)
            for cat, block, y0, y1, y2 in (
                (qcat, bq3, x[0:64], x[64:96], x[96:128]),
                (docat, bdo3, d[0:64], d1, d2),
            ):
                at = h * 256
                cat[pl.ds(at + 64 * blk, 64), :] = y0
                cat[pl.ds(at + 128 + 32 * blk, 32), :] = y1
                cat[pl.ds(at + 192 + 32 * blk, 32), :] = y2
                block[pl.ds(h * 128 + 32 * blk, 32), pl.ds(0, 128)] = y1
                block[pl.ds(h * 128 + 64 + 32 * blk, 32), pl.ds(128, 128)] = y2

    for cp in local[4:]:
        cp.wait()
    qx.wait_recv()
    dx.wait_recv()
    prepare(0)
    prepare(1)

    def gather_unit(u):
        for m in range(4 * u, 4 * u + 4):
            if m:
                pushes[m - 1].wait_recv()
        first = 4 * xor(duo, u)

        def rows(part, start, size):
            return jnp.concatenate(
                [kvg[first + b, part, pl.ds(start, size), :] for b in range(4)], 0
            )

        kp[u] = rows(0, 0, 64)
        vp[u] = rows(1, 0, 64)
        k3[u, :, 0:128] = rows(0, 64, 32)
        k3[u, :, 128:256] = rows(0, 96, 32)
        v3[u, :, 0:128] = rows(1, 64, 32)
        v3[u, :, 128:256] = rows(1, 96, 32)
        kt[:, pl.ds(256 * u, 256)] = kp[u].astype(F32).T.astype(BF16)
        kt3[:, pl.ds(128 * u, 128)] = k3[u].astype(F32).T.astype(BF16)

    def phase_a(u):
        gather_unit(u)
        earlier = xor(duo, u) < duo

        @pl.loop(0, HEADS)
        def _(h):
            at = pl.multiple_of(h * 256, 256)
            at3 = pl.multiple_of(h * 128, 128)
            rows = pl.ds(at, 256)
            rows3 = pl.ds(at3, 128)
            sc = dot_nt(kp[u], qcat[rows, :])
            if u == 0:
                sc = jnp.concatenate([sc[:, :128] + bias12[...], sc[:, 128:]], 1)
            top = jnp.max(sc, 0, keepdims=True)
            pr = jnp.exp2((sc - top) * C2)
            gp = dot_nt(vp[u], docat[rows, :])
            prob[u, :, rows] = pr
            gprob[u, :, rows] = gp
            if u:
                lane1 = lax.broadcasted_iota(jnp.int32, (1, 256), 1)
                top = jnp.where((lane1 >= 128) | earlier, top, NEG)
            st[u, 0:1, rows] = top
            st[u, 1:2, rows] = jnp.sum(pr, 0, keepdims=True)
            st[u, 2:3, rows] = jnp.sum(pr * gp, 0, keepdims=True)

            sc3 = dot_nt(k3[u], bq3[rows3, :]) + bias3[u]
            top3 = jnp.max(sc3, 0, keepdims=True)
            pr3 = jnp.exp2((sc3 - top3) * C2)
            gp3 = dot_nt(v3[u], bdo3[rows3, :])
            prob3[u, :, rows3] = pr3
            gprob3[u, :, rows3] = gp3
            st3[u, 0:1, rows3] = top3
            st3[u, 1:2, rows3] = jnp.sum(pr3, 0, keepdims=True)
            st3[u, 2:3, rows3] = jnp.sum(pr3 * gp3, 0, keepdims=True)

    for u in range(UNITS):
        phase_a(u)

    @pl.loop(0, HEADS)
    def _(h):
        rows = pl.ds(pl.multiple_of(h * 256, 256), 256)
        rows3 = pl.ds(pl.multiple_of(h * 128, 128), 128)
        zero = jnp.zeros((1, 128), F32)
        tops = [st[u, 0:1, rows] for u in range(UNITS)]
        tops3 = [st3[u, 0:1, rows3] for u in range(UNITS)]
        top = functools.reduce(jnp.maximum, tops)
        top_r = functools.reduce(jnp.maximum, tops3, top[:, 128:])
        top = jnp.concatenate([top[:, :128], top_r], 1)
        part = [jnp.exp2((t - top) * C2) for t in tops]
        part3 = [jnp.exp2((t - top_r) * C2) for t in tops3]
        total = sum(st[u, 1:2, rows] * part[u] for u in range(UNITS))
        total3 = sum(st3[u, 1:2, rows3] * part3[u] for u in range(UNITS))
        rdot = sum(st[u, 2:3, rows] * part[u] for u in range(UNITS))
        rdot3 = sum(st3[u, 2:3, rows3] * part3[u] for u in range(UNITS))
        inv = 1.0 / (total + jnp.concatenate([zero, total3], 1))
        rdot = (rdot + jnp.concatenate([zero, rdot3], 1)) * inv
        wrow[0:1, rows] = rdot
        for u in range(UNITS):
            st[u, 0:1, rows] = part[u] * inv
            st3[u, 0:1, rows3] = part3[u] * inv[:, 128:]

    sends = [None]
    vsum = jnp.zeros((1, 128), F32)
    back = {}
    for u in reversed(range(UNITS)):

        @pl.loop(0, HEADS)
        def _(h):
            at = pl.multiple_of(h * 256, 256)
            rows = pl.ds(at, 256)
            rows3 = pl.ds(pl.multiple_of(h * 128, 128), 128)
            rdot = wrow[0:1, rows]
            pr = prob[u, :, rows] * st[u, 0:1, rows]
            pb[:, rows] = pr.astype(BF16)
            dsb[pl.ds(256 * u, 256), rows] = (pr * (gprob[u, :, rows] - rdot)).astype(BF16)
            pr3 = prob3[u, :, rows3] * st3[u, 0:1, rows3]
            p3b[:, rows3] = pr3.astype(BF16)
            ds3b[pl.ds(128 * u, 128), rows3] = (
                pr3 * (gprob3[u, :, rows3] - rdot[:, 128:])
            ).astype(BF16)

        dv = dot(pb[...], docat[...])
        dv3 = dot(p3b[...], bdo3[...])
        dk = dot(dsb[pl.ds(256 * u, 256), :], qcat[...]) * SCALE
        dk3 = dot(ds3b[pl.ds(128 * u, 128), :], bq3[...]) * SCALE
        vsum = vsum + jnp.sum(dv, 0, keepdims=True)
        both = jnp.sum(dv3, 0, keepdims=True)
        vsum = vsum + both[:, :128] + both[:, 128:]
        for b in range(4):
            for col, big, small in ((0, dk, dk3), (128, dv, dv3)):
                cols = pl.ds(col, 128)
                stage[u, b, 0:64, cols] = big[64 * b : 64 * b + 64].astype(BF16)
                stage[u, b, 64:96, cols] = small[32 * b : 32 * b + 32, :128].astype(BF16)
                stage[u, b, 96:128, cols] = small[32 * b : 32 * b + 32, 128:].astype(BF16)
        for m in reversed(range(4 * u, 4 * u + 4)):
            if m:
                cp = remote(
                    stage.at[u, xor(s, m) % 4],
                    rs.at[m],
                    rs_send.at[m],
                    rs_recv.at[m],
                    seq_dev(m),
                )
                cp.start()
                back[m] = cp

    vec[7:8, :] = vsum
    lane = lax.broadcasted_iota(jnp.int32, (128, 128), 1)
    for h in range(HEADS):
        rows = pl.ds(h * 256, 256)
        rows3 = pl.ds(h * 128, 128)
        dqt = dot(kt[...], dsb[:, rows])
        dqt3 = dot(kt3[...], ds3b[:, rows3])
        right = dqt[:, 128:] + jnp.where(lane < 64, dqt3[:128], dqt3[128:])
        left = dqt[:, :128].T * SCALE
        right = right.T * SCALE
        vec[h : h + 1, :] = jnp.sum(left + right, 0, keepdims=True)
        cols = pl.ds(h * DIM, DIM)
        for blk in range(2):
            dqst[blk, 0:64, cols] = left[64 * blk : 64 * blk + 64]
            dqst[blk, 64:96, cols] = right[32 * blk : 32 * blk + 32]
            dqst[blk, 96:128, cols] = right[64 + 32 * blk : 96 + 32 * blk]

    step1 = []
    for k in range(1, 8):
        cp = remote(vec, ar1.at[k], a_send.at[k], a_recv.at[k], seq_dev(2 * k))
        cp.start()
        step1.append(cp)
    dq_far = remote(
        dqst.at[other], dq_hbm.at[:, own_cols], dq_sem.at[0], dq_sem.at[1], seq_dev(1)
    )
    dq_far.start()
    dq_own = pltpu.make_async_copy(dqst.at[core], dq_hbm.at[:, own_cols], dq_sem.at[2])
    dq_own.start()

    total = vec[...]
    for k in range(1, 8):
        step1[k - 1].wait_recv()
        total = total + ar1[k]
    ar1[0] = total
    started = list(step1)
    at = 8
    src = ar1.at[0]
    for group, buf in ((near, ar2), (far, ar3)):
        step = []
        for k, n in enumerate(group):
            cp = remote(src, buf.at[k + 1], a_send.at[at], a_recv.at[at], pair_dev(n))
            cp.start()
            step.append(cp)
            at += 1
        for k, cp in enumerate(step):
            cp.wait_recv()
            total = total + buf[k + 1]
        buf[0] = total
        src = buf.at[0]
        started += step
    last = remote(src, ar4, a_send.at[at], a_recv.at[at], seq_dev(1))
    last.start()
    started.append(last)

    mine = stage[0, s % 4].astype(F32)
    theirs = None
    for m in reversed(range(1, 16)):
        back[m].wait_recv()
        part = rs[m].astype(F32)
        if m % 2 == 0:
            mine = mine + part
        else:
            theirs = part if theirs is None else theirs + part
    for head, value in ((core, mine), (other, theirs)):
        dkv_ref[:, pl.ds(pl.multiple_of(head * 128, 128), 128)] = value[:, :128]
        dkv_ref[:, pl.ds(pl.multiple_of(256 + head * 128, 128), 128)] = value[:, 128:]

    last.wait_recv()
    sib = ar4[...]
    for head, value in ((core, total), (other, sib)):
        for h in range(HEADS):
            at = pl.multiple_of((head * HEADS + h) * DIM, 128)
            bq_ref[:, pl.ds(at, DIM)] = value[h : h + 1]
        bv_ref[:, pl.ds(pl.multiple_of(head * DIM, 128), DIM)] = value[7:8]

    dq_own.wait()
    dq_far.wait_recv()
    dq_far.wait_send()
    qx.wait_send()
    dx.wait_send()
    for cp in pushes + list(back.values()) + started:
        cp.wait_send()


def on_device(pairs, queries, keys_values, cotangent, resp_len, query_bias):
    near = [n for n in range(1, min(pairs, 4))]
    far = [n for n in range(4, pairs, 4)]
    vm = pltpu.VMEM
    dma = pltpu.SemaphoreType.DMA
    any_spec = pl.BlockSpec(memory_space=pl.ANY)
    vmem_spec = pl.BlockSpec(memory_space=pltpu.VMEM)
    scratch = [
        vm((2, 2, 128, 128), BF16),
        vm((16, 2, 128, 128), BF16),
        vm((2, 128, RLANES), BF16),
        vm((2, 128, RLANES), BF16),
        vm((LANES, 128), BF16),
        vm((LANES, 128), BF16),
        vm((RLANES, 256), BF16),
        vm((RLANES, 256), BF16),
        vm((UNITS, 256, 128), BF16),
        vm((UNITS, 256, 128), BF16),
        vm((UNITS, 128, 256), BF16),
        vm((UNITS, 128, 256), BF16),
        vm((128, UNITS * 256), BF16),
        vm((256, UNITS * 128), BF16),
        vm((256, 128), F32),
        vm((UNITS, 128, 128), F32),
        vm((UNITS, 256, LANES), F32),
        vm((UNITS, 256, LANES), F32),
        vm((UNITS, 128, RLANES), F32),
        vm((UNITS, 128, RLANES), F32),
        vm((UNITS, 8, LANES), F32),
        vm((UNITS, 8, RLANES), F32),
        vm((8, LANES), F32),
        vm((256, LANES), BF16),
        vm((UNITS * 256, LANES), BF16),
        vm((128, RLANES), BF16),
        vm((UNITS * 128, RLANES), BF16),
        vm((UNITS, 4, 128, 256), BF16),
        vm((16, 128, 256), BF16),
        vm((2, 128, RLANES), F32),
        vm((8, 128), F32),
        vm((8, 8, 128), F32),
        vm((len(near) + 1, 8, 128), F32),
        vm((len(far) + 1, 8, 128), F32),
        vm((8, 128), F32),
        dma((6,)),
        dma((16,)),
        dma((16,)),
        dma((2,)),
        dma((2,)),
        dma((16,)),
        dma((16,)),
        dma((3,)),
        dma((24,)),
        dma((24,)),
    ]
    dq, dkv, bq, bv = pl.pallas_call(
        functools.partial(kernel, near, far),
        out_shape=(
            jax.ShapeDtypeStruct((128, 2 * RLANES), F32),
            jax.ShapeDtypeStruct((128, 512), F32),
            jax.ShapeDtypeStruct((1, 2 * RLANES), F32),
            jax.ShapeDtypeStruct((1, 256), F32),
        ),
        in_specs=[
            any_spec,
            any_spec,
            any_spec,
            pl.BlockSpec(memory_space=pltpu.SMEM),
            vmem_spec,
        ],
        out_specs=(any_spec, vmem_spec, vmem_spec, vmem_spec),
        scratch_shapes=scratch,
        compiler_params=pltpu.CompilerParams(
            collective_id=0, has_side_effects=True, vmem_limit_bytes=50 * 1024 * 1024
        ),
    )(queries[0], keys_values[0], cotangent[0], resp_len, query_bias.reshape(1, -1))
    return dq[None], dkv[None], bq.reshape(-1), bv.reshape(-1)


def solution(mesh):
    return jax.shard_map(
        functools.partial(on_device, mesh.shape["pair"]),
        mesh=mesh,
        in_specs=(
            P("pair", "seq", None),
            P("pair", "seq", None),
            P("pair", "seq", None),
            P("pair", None),
            P(),
        ),
        out_specs=(P("pair", "seq", None), P("pair", "seq", None), P(), P()),
        check_vma=False,
    )
```

time: 422 us -> 73.8 us (0.17)
  waiting for transfers between devices: 130 us -> 0 us
  blocking collectives: 109 us -> 0 us
  starting transfers between devices: 66.9 us -> 0 us
  Pallas kernels: 0 us -> 66.5 us
  matrix products: 39.5 us -> 0 us
  other arithmetic: 33.2 us -> 0.62 us
  local copies, waits for them, and re-layouts: 25.3 us -> 5.83 us
  between operations: 14.2 us -> 0.66 us
    psum x1 -> x0, blocking collectives: 109 us -> none  [on_device(): lax.psum((grad_q.sum(0), grads[:, KEY_VALUE_HEADS * HEAD_SIZE:].sum(0)),...]
    ppermute x32 -> x0, waiting for transfers between devices: 85.8 us -> none  [passed_along(): lax.ppermute(shard, axis, [(i, (i + by) % count) for i in range(count)])]
    ppermute x32 -> x0, starting transfers between devices: 66.9 us -> none  [passed_along(): lax.ppermute(shard, axis, [(i, (i + by) % count) for i in range(count)])]
    pallas_call x0 -> x1, Pallas kernels: none -> 66.5 us  [on_device(): pl.pallas_call(functools.partial(kernel, near, far), out_shape=(jax.Shape...]
    all_gather x1 -> x0, waiting for transfers between devices: 44.6 us -> none  [on_device(): piece = lax.all_gather(kv_local, 'seq', axis=0, tiled=True)]
    dot_general x82 -> x0, matrix products: 39.5 us -> none  [the longest x17 9.84 us: block_scores(): jnp.einsum('qhgd,khd->qhgk', query_head_rows, key_rows, preferred_element...]
    lt x17 -> x0, other arithmetic: 21.7 us -> none  [visible(): k_place < k_limit]
    slice x34 -> x0, local copies, waits for them, and re-layouts: 12.7 us -> none  [the longest x17 10.8 us: visible(): k_limit = jnp.where(k_kind == 1, lengths[0], lengths[1])]
  transfers between devices with their start and end apart: 33 -> 0, of which waited for: 17 -> 0; matrix products, arithmetic and copies ran while one was open for 17% -> 0% of each run, Pallas kernels for 0% -> 0%
where the time goes in v1:
time: 73.8 us; the launch traced here: 73.6 us
  Pallas kernels  66.5 us (90%)
  local copies, waits for them, and re-layouts  5.83 us (8%)
    pallas_call x1, Pallas kernels, on_device(): pl.pallas_call(functools.partial(kernel, near, far), out_shape=(jax.Shape...  66.5 us
    unnamed x11, local copies, waits for them, and re-layouts  5.13 us

profile of v1, /device:TPU:1, one launch (start us, length us, event | category | flops | bytes accessed | tf_op | source)
XLA Modules:
  0.0 73.6 jit_solution(11287323806151116963)
XLA Ops:
  0.6 0.0 copy-start.3
  0.6 0.7 reshape.17.bias_ref
  1.3 0.0 copy-done.3
  1.4 0.0 copy-start
  1.4 1.0 %copy-done = bf16[1,128,1792]{2,1,0:T(8,128)(2,1)S(1)} copy-done((bf16[1,128,1792]{2,1,0:T(8,128)(2,1)S(1)}, bf16[1,128,1792]{2,1,0:T(8,128)(2,1)}, u32[]{:S(2)}) %copy-start) | copy-done | bytes 458776
  2.4 0.0 copy-start.1
  2.4 1.0 %copy-done.1 = bf16[1,128,1792]{2,1,0:T(8,128)(2,1)S(1)} copy-done((bf16[1,128,1792]{2,1,0:T(8,128)(2,1)S(1)}, bf16[1,128,1792]{2,1,0:T(8,128)(2,1)}, u32[]{:S(2)}) %copy-start.1) | copy-done | bytes 458776
  3.4 0.0 copy-start.2
  3.4 0.9 %copy-done.2 = bf16[1,128,512]{2,1,0:T(8,128)(2,1)S(1)} copy-done((bf16[1,128,512]{2,1,0:T(8,128)(2,1)S(1)}, bf16[1,128,512]{2,1,0:T(8,128)(2,1)}, u32[]{:S(2)}) %copy-start.2) | copy-done | bytes 131096
  4.3 66.5 %shard_map.84 = (f32[128,1792]{1,0:T(8,128)S(1)}, f32[128,512]{1,0:T(8,128)S(1)}, f32[1,1792]{1,0:T(1,128)S(1)}, f32[1,256]{1,0:T(1,128)S(1)}) custom-call(bf16[128,1792]{1,0:T(8,128)(2,1)S(1)} %bitcast.7, bf16[128,512]{1,0:T(8,128)(2,1)S(1)} %bitcast.10, bf16[128,1792]{1,0:T(8,128)(2,1)S(1)} %bitcast.8, s32[1,2]{1,0:T(1,128)S(1)} %copy-done.3, ...), custom_call_target="tpu_custom_call" | custom-call | tf_op jit(solution)/shard_map/pallas_call | solution.py:471
  70.8 0.6 reduce
  71.4 0.9 %copy.12 = f32[1,128,1792]{2,1,0:T(8,128)} copy(f32[1,128,1792]{2,1,0:T(8,128)S(1)} %bitcast.6) | data formatting | bytes 1835008
  72.3 0.7 copy.13
  73.0 0.6 copy.14
Async XLA Ops:
  0.6 0.7 copy-start.3
  1.4 1.0 %copy-start = (bf16[1,128,1792]{2,1,0:T(8,128)(2,1)S(1)}, bf16[1,128,1792]{2,1,0:T(8,128)(2,1)}, u32[]{:S(2)}) copy-start(bf16[1,128,1792]{2,1,0:T(8,128)(2,1)} %param.5) | copy-start | bytes 1376260
  2.4 1.0 %copy-start.1 = (bf16[1,128,1792]{2,1,0:T(8,128)(2,1)S(1)}, bf16[1,128,1792]{2,1,0:T(8,128)(2,1)}, u32[]{:S(2)}) copy-start(bf16[1,128,1792]{2,1,0:T(8,128)(2,1)} %param.7) | copy-start | bytes 1376260
  3.4 0.9 %copy-start.2 = (bf16[1,128,512]{2,1,0:T(8,128)(2,1)S(1)}, bf16[1,128,512]{2,1,0:T(8,128)(2,1)}, u32[]{:S(2)}) copy-start(bf16[1,128,512]{2,1,0:T(8,128)(2,1)} %param.6) | copy-start | bytes 393220

commit v2 on v1

--- a/solution.py
+++ b/solution.py
@@ -152,12 +152,15 @@
     dx = remote(cot_hbm.at[:, other_cols], doin.at[core], x_send.at[1], x_recv.at[1], seq_dev(1))
     qx.start()
     dx.start()
-    pushes = []
-    for m in range(1, 16):
-        head = xor(s, m) % 2
-        cp = remote(kvs.at[head], kvg.at[s], kv_send.at[m], kv_recv.at[m], seq_dev(m))
+    pushes = {}
+
+    def push(src, block, mask, to):
+        cp = remote(src, kvg.at[block], kv_send.at[mask], kv_recv.at[mask], seq_dev(to))
         cp.start()
-        pushes.append(cp)
+        pushes[mask] = cp
+
+    for m in (2, 3, 6, 7, 8, 9, 1):
+        push(kvs.at[xor(s, m) % 2], s, m, m)
     kvg[s] = kvs[core]
 
     len0, len1 = len_ref[0, 0], len_ref[0, 1]
@@ -181,7 +184,7 @@
         base = 32 * (2 * chip + blk)
         for h in range(HEADS):
             cols = pl.ds(h * DIM, DIM)
-            bias = bias_ref[:, pl.ds(pl.multiple_of((core * HEADS + h) * DIM, 128), DIM)]
+            bias = bias_ref[pl.ds(pl.multiple_of((core * HEADS + h) * DIM, 128), DIM)][None]
             x = (qin[blk, :, cols].astype(F32) + bias).astype(BF16)
             d = doin[blk, :, cols]
             d1 = jnp.where(row + base < len0, d[64:96].astype(F32), 0.0).astype(BF16)
@@ -204,10 +207,22 @@
     prepare(0)
     prepare(1)
 
+    arrivals = ((2, 3, 6, 7, 8, 9, 1), (4, 5), (10, 11), (12, 13, 14, 15))
+
+    def relay(mask, held, to):
+        push(kvg.at[xor(s, held)], xor(s, held), mask, to)
+
     def gather_unit(u):
-        for m in range(4 * u, 4 * u + 4):
-            if m:
-                pushes[m - 1].wait_recv()
+        for m in arrivals[u]:
+            pushes[m].wait_recv()
+        if u == 0:
+            relay(4, 2, 6)
+            relay(5, 7, 2)
+            for m, to in ((10, 2), (14, 6), (11, 2), (15, 6)):
+                relay(m, m - to, to)
+        elif u == 1:
+            relay(12, 4, 8)
+            relay(13, 5, 8)
         first = 4 * xor(duo, u)
 
         def rows(part, start, size):
@@ -228,7 +243,7 @@
         gather_unit(u)
         earlier = xor(duo, u) < duo
 
-        @pl.loop(0, HEADS)
+        @pl.loop(0, HEADS, unroll=True)
         def _(h):
             at = pl.multiple_of(h * 256, 256)
             at3 = pl.multiple_of(h * 128, 128)
@@ -285,114 +300,153 @@
             st[u, 0:1, rows] = part[u] * inv
             st3[u, 0:1, rows3] = part3[u] * inv[:, 128:]
 
-    sends = [None]
-    vsum = jnp.zeros((1, 128), F32)
-    back = {}
-    for u in reversed(range(UNITS)):
-
-        @pl.loop(0, HEADS)
+    def grad_scores(u):
+        @pl.loop(0, HEADS, unroll=True)
         def _(h):
             at = pl.multiple_of(h * 256, 256)
             rows = pl.ds(at, 256)
             rows3 = pl.ds(pl.multiple_of(h * 128, 128), 128)
             rdot = wrow[0:1, rows]
             pr = prob[u, :, rows] * st[u, 0:1, rows]
-            pb[:, rows] = pr.astype(BF16)
+            pb[u, :, rows] = pr.astype(BF16)
             dsb[pl.ds(256 * u, 256), rows] = (pr * (gprob[u, :, rows] - rdot)).astype(BF16)
             pr3 = prob3[u, :, rows3] * st3[u, 0:1, rows3]
-            p3b[:, rows3] = pr3.astype(BF16)
+            p3b[u, :, rows3] = pr3.astype(BF16)
             ds3b[pl.ds(128 * u, 128), rows3] = (
                 pr3 * (gprob3[u, :, rows3] - rdot[:, 128:])
             ).astype(BF16)
 
-        dv = dot(pb[...], docat[...])
-        dv3 = dot(p3b[...], bdo3[...])
+    def grad_kv(u):
+        dv = dot(pb[u], docat[...])
+        dv3 = dot(p3b[u], bdo3[...])
         dk = dot(dsb[pl.ds(256 * u, 256), :], qcat[...]) * SCALE
         dk3 = dot(ds3b[pl.ds(128 * u, 128), :], bq3[...]) * SCALE
-        vsum = vsum + jnp.sum(dv, 0, keepdims=True)
-        both = jnp.sum(dv3, 0, keepdims=True)
-        vsum = vsum + both[:, :128] + both[:, 128:]
         for b in range(4):
             for col, big, small in ((0, dk, dk3), (128, dv, dv3)):
                 cols = pl.ds(col, 128)
                 stage[u, b, 0:64, cols] = big[64 * b : 64 * b + 64].astype(BF16)
                 stage[u, b, 64:96, cols] = small[32 * b : 32 * b + 32, :128].astype(BF16)
                 stage[u, b, 96:128, cols] = small[32 * b : 32 * b + 32, 128:].astype(BF16)
-        for m in reversed(range(4 * u, 4 * u + 4)):
-            if m:
-                cp = remote(
-                    stage.at[u, xor(s, m) % 4],
-                    rs.at[m],
-                    rs_send.at[m],
-                    rs_recv.at[m],
-                    seq_dev(m),
-                )
-                cp.start()
-                back[m] = cp
-
-    vec[7:8, :] = vsum
-    lane = lax.broadcasted_iota(jnp.int32, (128, 128), 1)
-    for h in range(HEADS):
-        rows = pl.ds(h * 256, 256)
-        rows3 = pl.ds(h * 128, 128)
-        dqt = dot(kt[...], dsb[:, rows])
-        dqt3 = dot(kt3[...], ds3b[:, rows3])
-        right = dqt[:, 128:] + jnp.where(lane < 64, dqt3[:128], dqt3[128:])
-        left = dqt[:, :128].T * SCALE
-        right = right.T * SCALE
-        vec[h : h + 1, :] = jnp.sum(left + right, 0, keepdims=True)
-        cols = pl.ds(h * DIM, DIM)
-        for blk in range(2):
-            dqst[blk, 0:64, cols] = left[64 * blk : 64 * blk + 64]
-            dqst[blk, 64:96, cols] = right[32 * blk : 32 * blk + 32]
-            dqst[blk, 96:128, cols] = right[64 + 32 * blk : 96 + 32 * blk]
-
+
+    back = []
+
+    def part(m):
+        return stage.at[m // 4, xor(s, m) % 4]
+
+    def give(m, slot, to):
+        cp = remote(part(m), rs.at[slot], rs_send.at[slot], rs_recv.at[slot], seq_dev(to))
+        cp.start()
+        back.append(cp)
+
+    def landed(slot):
+        remote(
+            rs.at[slot], rs.at[slot], rs_send.at[slot], rs_recv.at[slot], seq_dev(1)
+        ).wait_recv()
+
+    def add(m, *slots):
+        total = part(m)[...].astype(F32)
+        for slot in slots:
+            landed(slot)
+            total = total + rs[slot].astype(F32)
+        part(m)[...] = total.astype(BF16)
+
+    def grad_queries():
+        lane = lax.broadcasted_iota(jnp.int32, (128, 128), 1)
+        for h in range(HEADS):
+            rows = pl.ds(h * 256, 256)
+            rows3 = pl.ds(h * 128, 128)
+            dqt = dot(kt[...], dsb[:, rows])
+            dqt3 = dot(kt3[...], ds3b[:, rows3])
+            right = dqt[:, 128:] + jnp.where(lane < 64, dqt3[:128], dqt3[128:])
+            left = dqt[:, :128].T * SCALE
+            right = right.T * SCALE
+            vec[h : h + 1, :] = jnp.sum(left + right, 0, keepdims=True)
+            cols = pl.ds(h * DIM, DIM)
+            for blk in range(2):
+                dqst[blk, 0:64, cols] = left[64 * blk : 64 * blk + 64]
+                dqst[blk, 64:96, cols] = right[32 * blk : 32 * blk + 32]
+                dqst[blk, 96:128, cols] = right[64 + 32 * blk : 96 + 32 * blk]
+
+    grad_scores(3)
+    grad_kv(3)
+    give(12, 0, 8)
+    give(14, 2, 6)
+    give(13, 1, 8)
+    give(15, 3, 6)
+    for u in (2, 1, 0):
+        grad_scores(u)
+    grad_queries()
+    vec[7:8, :] = dot(jnp.ones((8, LANES), BF16), docat[...])[0:1]
     step1 = []
     for k in range(1, 8):
         cp = remote(vec, ar1.at[k], a_send.at[k], a_recv.at[k], seq_dev(2 * k))
         cp.start()
         step1.append(cp)
+    grad_kv(2)
+    give(10, 4, 2)
+    give(11, 5, 2)
+    grad_kv(1)
+    give(6, 6, 6)
     dq_far = remote(
         dqst.at[other], dq_hbm.at[:, own_cols], dq_sem.at[0], dq_sem.at[1], seq_dev(1)
     )
     dq_far.start()
     dq_own = pltpu.make_async_copy(dqst.at[core], dq_hbm.at[:, own_cols], dq_sem.at[2])
     dq_own.start()
-
+    add(4, 0)
+    give(4, 7, 6)
+    add(5, 1)
+    give(5, 8, 2)
     total = vec[...]
     for k in range(1, 8):
         step1[k - 1].wait_recv()
         total = total + ar1[k]
     ar1[0] = total
     started = list(step1)
-    at = 8
-    src = ar1.at[0]
-    for group, buf in ((near, ar2), (far, ar3)):
+
+    def to_pairs(group, buf, at, src):
         step = []
         for k, n in enumerate(group):
-            cp = remote(src, buf.at[k + 1], a_send.at[at], a_recv.at[at], pair_dev(n))
+            cp = remote(src, buf.at[k + 1], a_send.at[at + k], a_recv.at[at + k], pair_dev(n))
             cp.start()
             step.append(cp)
-            at += 1
+        started.extend(step)
+        return step
+
+    def from_pairs(step, buf, total):
         for k, cp in enumerate(step):
             cp.wait_recv()
             total = total + buf[k + 1]
         buf[0] = total
-        src = buf.at[0]
-        started += step
-    last = remote(src, ar4, a_send.at[at], a_recv.at[at], seq_dev(1))
+        return total
+
+    step2 = to_pairs(near, ar2, 8, ar1.at[0])
+    grad_kv(0)
+    give(3, 9, 3)
+    give(1, 10, 1)
+    add(8, 2, 4)
+    give(8, 11, 8)
+    add(9, 3, 5)
+    give(9, 12, 9)
+    total = from_pairs(step2, ar2, total)
+    step3 = to_pairs(far, ar3, 11, ar2.at[0])
+    add(2, 7)
+    give(2, 13, 2)
+    add(7, 8)
+    give(7, 14, 7)
+    total = from_pairs(step3, ar3, total)
+    last = remote(ar3.at[0], ar4, a_send.at[18], a_recv.at[18], seq_dev(1))
     last.start()
     started.append(last)
 
-    mine = stage[0, s % 4].astype(F32)
-    theirs = None
-    for m in reversed(range(1, 16)):
-        back[m].wait_recv()
-        part = rs[m].astype(F32)
-        if m % 2 == 0:
-            mine = mine + part
-        else:
-            theirs = part if theirs is None else theirs + part
+    mine = part(0)[...].astype(F32)
+    for slot in (6, 11, 13):
+        landed(slot)
+        mine = mine + rs[slot].astype(F32)
+    theirs = jnp.zeros((128, 256), F32)
+    for slot in (10, 9, 12, 14):
+        landed(slot)
+        theirs = theirs + rs[slot].astype(F32)
     for head, value in ((core, mine), (other, theirs)):
         dkv_ref[:, pl.ds(pl.multiple_of(head * 128, 128), 128)] = value[:, :128]
         dkv_ref[:, pl.ds(pl.multiple_of(256 + head * 128, 128), 128)] = value[:, 128:]
@@ -402,16 +456,25 @@
     for head, value in ((core, total), (other, sib)):
         for h in range(HEADS):
             at = pl.multiple_of((head * HEADS + h) * DIM, 128)
-            bq_ref[:, pl.ds(at, DIM)] = value[h : h + 1]
-        bv_ref[:, pl.ds(pl.multiple_of(head * DIM, 128), DIM)] = value[7:8]
+            bq_ref[pl.ds(at, DIM)] = value[h]
+        bv_ref[pl.ds(pl.multiple_of(head * DIM, 128), DIM)] = value[7]
 
     dq_own.wait()
     dq_far.wait_recv()
     dq_far.wait_send()
     qx.wait_send()
     dx.wait_send()
-    for cp in pushes + list(back.values()) + started:
+    for cp in list(pushes.values()) + back + started:
         cp.wait_send()
+
+
+def hand_out(*refs):
+    ins, outs, sem = refs[:4], refs[4:8], refs[8]
+    copies = [pltpu.make_async_copy(a, b, sem.at[i]) for i, (a, b) in enumerate(zip(ins, outs))]
+    for cp in copies:
+        cp.start()
+    for cp in copies:
+        cp.wait()
 
 
 def on_device(pairs, queries, keys_values, cotangent, resp_len, query_bias):
@@ -420,6 +483,7 @@
     vm = pltpu.VMEM
     dma = pltpu.SemaphoreType.DMA
     any_spec = pl.BlockSpec(memory_space=pl.ANY)
+    hbm_spec = pl.BlockSpec(memory_space=pltpu.HBM)
     vmem_spec = pl.BlockSpec(memory_space=pltpu.VMEM)
     scratch = [
         vm((2, 2, 128, 128), BF16),
@@ -445,9 +509,9 @@
         vm((UNITS, 8, LANES), F32),
         vm((UNITS, 8, RLANES), F32),
         vm((8, LANES), F32),
-        vm((256, LANES), BF16),
+        vm((UNITS, 256, LANES), BF16),
         vm((UNITS * 256, LANES), BF16),
-        vm((128, RLANES), BF16),
+        vm((UNITS, 128, RLANES), BF16),
         vm((UNITS * 128, RLANES), BF16),
         vm((UNITS, 4, 128, 256), BF16),
         vm((16, 128, 256), BF16),
@@ -468,28 +532,36 @@
         dma((24,)),
         dma((24,)),
     ]
-    dq, dkv, bq, bv = pl.pallas_call(
+    shapes = (
+        jax.ShapeDtypeStruct((128, 2 * RLANES), F32),
+        jax.ShapeDtypeStruct((128, 512), F32),
+        jax.ShapeDtypeStruct((2 * RLANES,), F32),
+        jax.ShapeDtypeStruct((256,), F32),
+    )
+    made = pl.pallas_call(
         functools.partial(kernel, near, far),
-        out_shape=(
-            jax.ShapeDtypeStruct((128, 2 * RLANES), F32),
-            jax.ShapeDtypeStruct((128, 512), F32),
-            jax.ShapeDtypeStruct((1, 2 * RLANES), F32),
-            jax.ShapeDtypeStruct((1, 256), F32),
-        ),
+        out_shape=shapes,
         in_specs=[
-            any_spec,
-            any_spec,
-            any_spec,
+            hbm_spec,
+            hbm_spec,
+            hbm_spec,
             pl.BlockSpec(memory_space=pltpu.SMEM),
             vmem_spec,
         ],
         out_specs=(any_spec, vmem_spec, vmem_spec, vmem_spec),
         scratch_shapes=scratch,
         compiler_params=pltpu.CompilerParams(
-            collective_id=0, has_side_effects=True, vmem_limit_bytes=50 * 1024 * 1024
+            collective_id=0, has_side_effects=True, vmem_limit_bytes=63 * 1024 * 1024
         ),
-    )(queries[0], keys_values[0], cotangent[0], resp_len, query_bias.reshape(1, -1))
-    return dq[None], dkv[None], bq.reshape(-1), bv.reshape(-1)
+    )(queries[0], keys_values[0], cotangent[0], resp_len, query_bias)
+    dq, dkv, bq, bv = pl.pallas_call(
+        hand_out,
+        out_shape=shapes,
+        in_specs=[vmem_spec] * 4,
+        out_specs=(any_spec,) * 4,
+        scratch_shapes=[dma((4,))],
+    )(*made)
+    return dq[None], dkv[None], bq, bv
 
 
 def solution(mesh):

time: 73.8 us -> 55.8 us (0.76)
  Pallas kernels: 66.5 us -> 54.9 us
  local copies, waits for them, and re-layouts: 5.83 us -> 0 us
    pallas_call x1 -> x2, Pallas kernels: 66.5 us -> 54.9 us  [the longest x1 52.6 us: on_device(): pl.pallas_call(functools.partial(kernel, near, far), out_shape=shapes, in...]
    unnamed x11 -> x0, local copies, waits for them, and re-layouts: 5.13 us -> none
where the time goes in v2:
time: 55.8 us; the launch traced here: 55.6 us
  Pallas kernels  54.9 us (98%)
  between operations  0.64 us (1%)
    pallas_call x1, Pallas kernels, on_device(): pl.pallas_call(functools.partial(kernel, near, far), out_shape=shapes, in...  52.6 us
    pallas_call x1, Pallas kernels, on_device(): pl.pallas_call(hand_out, out_shape=shapes, in_specs=[vmem_spec] * 4, out_...  2.31 us

profile of v2, /device:TPU:1, one launch (start us, length us, event | category | flops | bytes accessed | tf_op | source)
XLA Modules:
  0.0 55.6 jit_solution(16770400523022653706)
XLA Ops:
  0.6 52.6 %shard_map.84 = (f32[128,1792]{1,0:T(8,128)}, f32[128,512]{1,0:T(8,128)}, f32[1792]{0:T(1024)}, f32[256]{0:T(256)}) custom-call(bf16[128,1792]{1,0:T(8,128)(2,1)} %bitcast.5, bf16[128,512]{1,0:T(8,128)(2,1)} %bitcast.7, bf16[128,1792]{1,0:T(8,128)(2,1)} %bitcast.6, s32[1,2]{1,0:T(1,128)} %len_ref.1, f32[1792]{0:T(1024)} %bias_ref.1), custom_call_target="tpu_custom_call" | custom-call | tf_op jit(solution)/shard_map/pallas_call | solution.py:541
  53.3 2.3 %shard_map.85 = (f32[128,1792]{1,0:T(8,128)}, f32[128,512]{1,0:T(8,128)}, f32[1792]{0:T(1024)}, f32[256]{0:T(256)}) custom-call(f32[128,1792]{1,0:T(8,128)} %get-tuple-element.12.refs_0_, f32[128,512]{1,0:T(8,128)} %get-tuple-element.13.refs_1_, f32[1792]{0:T(1024)} %get-tuple-element.14.refs_2_, f32[256]{0:T(256)} %get-tuple-element.15.refs_3_), custom_call_target="tpu_custom_call" | custom-call | tf_op jit(solution)/shard_map/pallas_call | solution.py:557

commit v3 on v2

--- a/solution.py
+++ b/solution.py
@@ -45,8 +45,8 @@
     q_hbm,
     kv_hbm,
     cot_hbm,
-    len_ref,
-    bias_ref,
+    len_hbm,
+    bias_hbm,
     dq_hbm,
     dkv_ref,
     bq_ref,
@@ -85,7 +85,9 @@
     ar1,
     ar2,
     ar3,
-    ar4,
+    res,
+    len_ref,
+    bias_ref,
     loc_sem,
     kv_send,
     kv_recv,
@@ -96,6 +98,8 @@
     dq_sem,
     a_send,
     a_recv,
+    b_recv,
+    go_sem,
 ):
     s = lax.axis_index("seq")
     p = lax.axis_index("pair")
@@ -126,17 +130,36 @@
             )
     local.append(pltpu.make_async_copy(q_hbm.at[:, own_cols], qin.at[core], loc_sem.at[4]))
     local.append(pltpu.make_async_copy(cot_hbm.at[:, own_cols], doin.at[core], loc_sem.at[5]))
+    local.append(pltpu.make_async_copy(bias_hbm, bias_ref, loc_sem.at[6]))
+    local.append(pltpu.make_async_copy(len_hbm, len_ref, loc_sem.at[7]))
     for cp in local:
         cp.start()
 
     barrier = pltpu.get_barrier_semaphore()
-    for m in range(1, 16):
-        pl.semaphore_signal(barrier, inc=1, device_id=seq_dev(m), device_id_type=MESH)
-    for n in near + far:
-        pl.semaphore_signal(barrier, inc=1, device_id=pair_dev(n), device_id_type=MESH)
+
+    @pl.when(core == 0)
+    def _():
+        for m in (2, 6, 8):
+            pl.semaphore_signal(barrier, inc=1, device_id=seq_dev(m), device_id_type=MESH)
+
+    @pl.when(core == 1)
+    def _():
+        for m in (3, 7, 9, 1):
+            pl.semaphore_signal(barrier, inc=1, device_id=seq_dev(m), device_id_type=MESH)
+        for n in near + far:
+            pl.semaphore_signal(barrier, inc=1, device_id=pair_dev(n), device_id_type=MESH)
+
     for cp in local[:4]:
         cp.wait()
-    pl.semaphore_wait(barrier, 15 + len(near) + len(far))
+
+    @pl.when(core == 0)
+    def _():
+        pl.semaphore_wait(barrier, 7)
+        pl.semaphore_signal(go_sem, inc=1, device_id=seq_dev(1), device_id_type=MESH)
+
+    @pl.when(core == 1)
+    def _():
+        pl.semaphore_wait(go_sem, 1)
 
     def remote(src, dst, send, recv, dev):
         return pltpu.make_async_remote_copy(
@@ -148,21 +171,22 @@
             device_id_type=MESH,
         )
 
+    pushes = {}
+
+    def push(src, block, mask, to):
+        cp = remote(src, kvg.at[block], kv_send.at[mask], kv_recv.at[mask], seq_dev(to))
+        cp.start()
+        pushes[mask] = cp
+
+    for m in (2, 7, 8, 3, 6, 9, 1):
+        push(kvs.at[xor(s, m) % 2], s, m, m)
     qx = remote(q_hbm.at[:, other_cols], qin.at[core], x_send.at[0], x_recv.at[0], seq_dev(1))
     dx = remote(cot_hbm.at[:, other_cols], doin.at[core], x_send.at[1], x_recv.at[1], seq_dev(1))
     qx.start()
     dx.start()
-    pushes = {}
-
-    def push(src, block, mask, to):
-        cp = remote(src, kvg.at[block], kv_send.at[mask], kv_recv.at[mask], seq_dev(to))
-        cp.start()
-        pushes[mask] = cp
-
-    for m in (2, 3, 6, 7, 8, 9, 1):
-        push(kvs.at[xor(s, m) % 2], s, m, m)
     kvg[s] = kvs[core]
 
+    local[7].wait()
     len0, len1 = len_ref[0, 0], len_ref[0, 1]
     key = lax.broadcasted_iota(jnp.int32, (256, 128), 0)
     lane = lax.broadcasted_iota(jnp.int32, (256, 128), 1)
@@ -194,35 +218,33 @@
                 (docat, bdo3, d[0:64], d1, d2),
             ):
                 at = h * 256
-                cat[pl.ds(at + 64 * blk, 64), :] = y0
-                cat[pl.ds(at + 128 + 32 * blk, 32), :] = y1
-                cat[pl.ds(at + 192 + 32 * blk, 32), :] = y2
-                block[pl.ds(h * 128 + 32 * blk, 32), pl.ds(0, 128)] = y1
-                block[pl.ds(h * 128 + 64 + 32 * blk, 32), pl.ds(128, 128)] = y2
-
-    for cp in local[4:]:
-        cp.wait()
+                cat[pl.ds(pl.multiple_of(at + 64 * blk, 64), 64), :] = y0
+                cat[pl.ds(pl.multiple_of(at + 128 + 32 * blk, 32), 32), :] = y1
+                cat[pl.ds(pl.multiple_of(at + 192 + 32 * blk, 32), 32), :] = y2
+                block[pl.ds(pl.multiple_of(h * 128 + 32 * blk, 32), 32), pl.ds(0, 128)] = y1
+                block[pl.ds(pl.multiple_of(h * 128 + 64 + 32 * blk, 32), 32), pl.ds(128, 128)] = y2
+
+    def relay(held, *ways):
+        pushes[held].wait_recv()
+        for mask, to in ways:
+            push(kvg.at[xor(s, held)], xor(s, held), mask, to)
+
+    relay(2, (4, 6))
+    relay(7, (5, 2))
+    for k in (4, 5, 6):
+        local[k].wait()
+    prepare(core)
+    relay(8, (10, 2), (14, 6))
+    relay(9, (11, 2), (15, 6))
     qx.wait_recv()
     dx.wait_recv()
-    prepare(0)
-    prepare(1)
-
-    arrivals = ((2, 3, 6, 7, 8, 9, 1), (4, 5), (10, 11), (12, 13, 14, 15))
-
-    def relay(mask, held, to):
-        push(kvg.at[xor(s, held)], xor(s, held), mask, to)
+    prepare(other)
+    more = {0: ((3,), (6,), (1,)), 1: ((4, (12, 8)), (5, (13, 8))), 2: ((10,), (11,))}
+    more[3] = ((12,), (13,), (14,), (15,))
 
     def gather_unit(u):
-        for m in arrivals[u]:
-            pushes[m].wait_recv()
-        if u == 0:
-            relay(4, 2, 6)
-            relay(5, 7, 2)
-            for m, to in ((10, 2), (14, 6), (11, 2), (15, 6)):
-                relay(m, m - to, to)
-        elif u == 1:
-            relay(12, 4, 8)
-            relay(13, 5, 8)
+        for way in more[u]:
+            relay(*way)
         first = 4 * xor(duo, u)
 
         def rows(part, start, size):
@@ -377,16 +399,57 @@
         grad_scores(u)
     grad_queries()
     vec[7:8, :] = dot(jnp.ones((8, LANES), BF16), docat[...])[0:1]
-    step1 = []
+    sums = []
+    for k in range(8):
+        sums.append(
+            remote(
+                vec,
+                ar1.at[k, core],
+                a_send.at[k],
+                a_recv.at[2 * k + core],
+                {"seq": xor(s, 2 * k) + 1 - core, "pair": p},
+            )
+        )
     for k in range(1, 8):
-        cp = remote(vec, ar1.at[k], a_send.at[k], a_recv.at[k], seq_dev(2 * k))
-        cp.start()
-        step1.append(cp)
+        sums[k].start()
+
+    @pl.when(core == 0)
+    def _():
+        sums[0].start()
+
+    def pair_step(group, buf, at):
+        return [
+            remote(buf.at[0], buf.at[k + 1], a_send.at[at + k], b_recv.at[at + k], pair_dev(n))
+            for k, n in enumerate(group)
+        ]
+
+    near_step, far_step = pair_step(near, ar2, 8), pair_step(far, ar3, 11)
+    last = remote(res, res, a_send.at[18], b_recv.at[18], seq_dev(1))
+
     grad_kv(2)
     give(10, 4, 2)
     give(11, 5, 2)
     grad_kv(1)
     give(6, 6, 6)
+
+    @pl.when(core == 1)
+    def _():
+        total = [None, vec[...]]
+        for k in range(8):
+            for c in range(2):
+                if (k, c) == (0, 1):
+                    continue
+                remote(
+                    vec, ar1.at[k, c], a_send.at[k], a_recv.at[2 * k + c], seq_dev(1)
+                ).wait_recv()
+                total[c] = ar1[k, c] if total[c] is None else total[c] + ar1[k, c]
+        ar2[0, 0] = total[0]
+        ar2[0, 1] = total[1]
+        if near:
+            pl.semaphore_wait(barrier, len(near) + len(far))
+        for cp in near_step:
+            cp.start()
+
     dq_far = remote(
         dqst.at[other], dq_hbm.at[:, own_cols], dq_sem.at[0], dq_sem.at[1], seq_dev(1)
     )
@@ -397,47 +460,37 @@
     give(4, 7, 6)
     add(5, 1)
     give(5, 8, 2)
-    total = vec[...]
-    for k in range(1, 8):
-        step1[k - 1].wait_recv()
-        total = total + ar1[k]
-    ar1[0] = total
-    started = list(step1)
-
-    def to_pairs(group, buf, at, src):
-        step = []
-        for k, n in enumerate(group):
-            cp = remote(src, buf.at[k + 1], a_send.at[at + k], a_recv.at[at + k], pair_dev(n))
-            cp.start()
-            step.append(cp)
-        started.extend(step)
-        return step
-
-    def from_pairs(step, buf, total):
-        for k, cp in enumerate(step):
-            cp.wait_recv()
-            total = total + buf[k + 1]
-        buf[0] = total
-        return total
-
-    step2 = to_pairs(near, ar2, 8, ar1.at[0])
     grad_kv(0)
     give(3, 9, 3)
     give(1, 10, 1)
+
+    @pl.when(core == 1)
+    def _():
+        total = ar2[0]
+        for k, cp in enumerate(near_step):
+            cp.wait_recv()
+            total = total + ar2[k + 1]
+        ar3[0] = total
+        for cp in far_step:
+            cp.start()
+
     add(8, 2, 4)
     give(8, 11, 8)
     add(9, 3, 5)
     give(9, 12, 9)
-    total = from_pairs(step2, ar2, total)
-    step3 = to_pairs(far, ar3, 11, ar2.at[0])
     add(2, 7)
     give(2, 13, 2)
     add(7, 8)
     give(7, 14, 7)
-    total = from_pairs(step3, ar3, total)
-    last = remote(ar3.at[0], ar4, a_send.at[18], a_recv.at[18], seq_dev(1))
-    last.start()
-    started.append(last)
+
+    @pl.when(core == 1)
+    def _():
+        total = ar3[0]
+        for k, cp in enumerate(far_step):
+            cp.wait_recv()
+            total = total + ar3[k + 1]
+        res[...] = total
+        last.start()
 
     mine = part(0)[...].astype(F32)
     for slot in (6, 11, 13):
@@ -451,21 +504,31 @@
         dkv_ref[:, pl.ds(pl.multiple_of(head * 128, 128), 128)] = value[:, :128]
         dkv_ref[:, pl.ds(pl.multiple_of(256 + head * 128, 128), 128)] = value[:, 128:]
 
-    last.wait_recv()
-    sib = ar4[...]
-    for head, value in ((core, total), (other, sib)):
+    @pl.when(core == 0)
+    def _():
+        last.wait_recv()
+
+    for head in range(2):
         for h in range(HEADS):
-            at = pl.multiple_of((head * HEADS + h) * DIM, 128)
-            bq_ref[pl.ds(at, DIM)] = value[h]
-        bv_ref[pl.ds(pl.multiple_of(head * DIM, 128), DIM)] = value[7]
+            bq_ref[pl.ds((head * HEADS + h) * DIM, DIM)] = res[head, h]
+        bv_ref[pl.ds(head * DIM, DIM)] = res[head, 7]
 
     dq_own.wait()
     dq_far.wait_recv()
     dq_far.wait_send()
     qx.wait_send()
     dx.wait_send()
-    for cp in list(pushes.values()) + back + started:
+    for cp in list(pushes.values()) + back + sums[1:]:
         cp.wait_send()
+
+    @pl.when(core == 0)
+    def _():
+        sums[0].wait_send()
+
+    @pl.when(core == 1)
+    def _():
+        for cp in near_step + far_step + [last]:
+            cp.wait_send()
 
 
 def hand_out(*refs):
@@ -517,11 +580,13 @@
         vm((16, 128, 256), BF16),
         vm((2, 128, RLANES), F32),
         vm((8, 128), F32),
-        vm((8, 8, 128), F32),
-        vm((len(near) + 1, 8, 128), F32),
-        vm((len(far) + 1, 8, 128), F32),
-        vm((8, 128), F32),
-        dma((6,)),
+        vm((8, 2, 8, 128), F32),
+        vm((len(near) + 1, 2, 8, 128), F32),
+        vm((len(far) + 1, 2, 8, 128), F32),
+        vm((2, 8, 128), F32),
+        pltpu.SMEM((1, 2), jnp.int32),
+        vm((2 * RLANES,), F32),
+        dma((8,)),
         dma((16,)),
         dma((16,)),
         dma((2,)),
@@ -529,8 +594,10 @@
         dma((16,)),
         dma((16,)),
         dma((3,)),
-        dma((24,)),
-        dma((24,)),
+        dma((19,)),
+        dma((16,)),
+        dma((19,)),
+        pltpu.SemaphoreType.REGULAR,
     ]
     shapes = (
         jax.ShapeDtypeStruct((128, 2 * RLANES), F32),
@@ -545,8 +612,8 @@
             hbm_spec,
             hbm_spec,
             hbm_spec,
-            pl.BlockSpec(memory_space=pltpu.SMEM),
-            vmem_spec,
+            hbm_spec,
+            hbm_spec,
         ],
         out_specs=(any_spec, vmem_spec, vmem_spec, vmem_spec),
         scratch_shapes=scratch,

time: 55.8 us -> 51.1 us (0.916)
  Pallas kernels: 54.9 us -> 50.3 us
    pallas_call x1, Pallas kernels: 52.6 us -> 48 us  [on_device(): pl.pallas_call(functools.partial(kernel, near, far), out_shape=shapes, in...]
where the time goes in v3:
time: 51.1 us; the launch traced here: 51 us
  Pallas kernels  50.3 us (98%)
  between operations  0.64 us (1%)
    pallas_call x1, Pallas kernels, on_device(): pl.pallas_call(functools.partial(kernel, near, far), out_shape=shapes, in...  48 us
    pallas_call x1, Pallas kernels, on_device(): pl.pallas_call(hand_out, out_shape=shapes, in_specs=[vmem_spec] * 4, out_...  2.31 us

profile of v3, /device:TPU:1, one launch (start us, length us, event | category | flops | bytes accessed | tf_op | source)
XLA Modules:
  0.0 51.0 jit_solution(9319450944203319856)
XLA Ops:
  0.6 48.0 %shard_map.84 = (f32[128,1792]{1,0:T(8,128)}, f32[128,512]{1,0:T(8,128)}, f32[1792]{0:T(1024)}, f32[256]{0:T(256)}) custom-call(bf16[128,1792]{1,0:T(8,128)(2,1)} %bitcast.5, bf16[128,512]{1,0:T(8,128)(2,1)} %bitcast.7, bf16[128,1792]{1,0:T(8,128)(2,1)} %bitcast.6, s32[1,2]{1,0:T(1,128)} %len_hbm.1, f32[1792]{0:T(1024)} %bias_hbm.1), custom_call_target="tpu_custom_call" | custom-call | tf_op jit(solution)/shard_map/pallas_call | solution.py:608
  48.7 2.3 %shard_map.85 = (f32[128,1792]{1,0:T(8,128)}, f32[128,512]{1,0:T(8,128)}, f32[1792]{0:T(1024)}, f32[256]{0:T(256)}) custom-call(f32[128,1792]{1,0:T(8,128)} %get-tuple-element.12.refs_0_, f32[128,512]{1,0:T(8,128)} %get-tuple-element.13.refs_1_, f32[1792]{0:T(1024)} %get-tuple-element.14.refs_2_, f32[256]{0:T(256)} %get-tuple-element.15.refs_3_), custom_call_target="tpu_custom_call" | custom-call | tf_op jit(solution)/shard_map/pallas_call | solution.py:624

commit v4 on v3

--- a/solution.py
+++ b/solution.py
@@ -40,8 +40,7 @@
 
 
 def kernel(
-    pair_near,
-    pair_far,
+    pairs,
     q_hbm,
     kv_hbm,
     cot_hbm,
@@ -84,7 +83,6 @@
     vec,
     ar1,
     ar2,
-    ar3,
     res,
     len_ref,
     bias_ref,
@@ -98,7 +96,10 @@
     dq_sem,
     a_send,
     a_recv,
+    b_send,
     b_recv,
+    c_send,
+    c_recv,
     go_sem,
 ):
     s = lax.axis_index("seq")
@@ -107,7 +108,6 @@
     core = s % 2
     other = 1 - core
     duo = s // 4
-    near, far = pair_near, pair_far
 
     def seq_dev(m):
         return {"seq": xor(s, m), "pair": p}
@@ -146,8 +146,6 @@
     def _():
         for m in (3, 7, 9, 1):
             pl.semaphore_signal(barrier, inc=1, device_id=seq_dev(m), device_id_type=MESH)
-        for n in near + far:
-            pl.semaphore_signal(barrier, inc=1, device_id=pair_dev(n), device_id_type=MESH)
 
     for cp in local[:4]:
         cp.wait()
@@ -184,6 +182,12 @@
     dx = remote(cot_hbm.at[:, other_cols], doin.at[core], x_send.at[1], x_recv.at[1], seq_dev(1))
     qx.start()
     dx.start()
+
+    @pl.when(core == 1)
+    def _():
+        for n in range(1, pairs):
+            pl.semaphore_signal(barrier, inc=1, device_id=pair_dev(n), device_id_type=MESH)
+
     kvg[s] = kvs[core]
 
     local[7].wait()
@@ -382,7 +386,7 @@
             right = dqt[:, 128:] + jnp.where(lane < 64, dqt3[:128], dqt3[128:])
             left = dqt[:, :128].T * SCALE
             right = right.T * SCALE
-            vec[h : h + 1, :] = jnp.sum(left + right, 0, keepdims=True)
+            vec[h] = jnp.sum(left + right, 0, keepdims=True)
             cols = pl.ds(h * DIM, DIM)
             for blk in range(2):
                 dqst[blk, 0:64, cols] = left[64 * blk : 64 * blk + 64]
@@ -398,12 +402,12 @@
     for u in (2, 1, 0):
         grad_scores(u)
     grad_queries()
-    vec[7:8, :] = dot(jnp.ones((8, LANES), BF16), docat[...])[0:1]
+    vec[7] = dot(jnp.ones((8, LANES), BF16), docat[...])[0:1]
     sums = []
     for k in range(8):
         sums.append(
             remote(
-                vec,
+                vec.at[xor(s, 2 * k) // 2],
                 ar1.at[k, core],
                 a_send.at[k],
                 a_recv.at[2 * k + core],
@@ -417,38 +421,40 @@
     def _():
         sums[0].start()
 
-    def pair_step(group, buf, at):
-        return [
-            remote(buf.at[0], buf.at[k + 1], a_send.at[at + k], b_recv.at[at + k], pair_dev(n))
-            for k, n in enumerate(group)
-        ]
-
-    near_step, far_step = pair_step(near, ar2, 8), pair_step(far, ar3, 11)
-    last = remote(res, res, a_send.at[18], b_recv.at[18], seq_dev(1))
+    pair_step = [
+        remote(ar2.at[0], ar2.at[n], b_send.at[n], b_recv.at[n], pair_dev(n))
+        for n in range(1, pairs)
+    ]
+    spread = [
+        remote(res.at[chip], res.at[chip], c_send.at[m], c_recv.at[m // 2], seq_dev(m))
+        for m in range(1, 16)
+    ]
 
     grad_kv(2)
     give(10, 4, 2)
     give(11, 5, 2)
+
     grad_kv(1)
     give(6, 6, 6)
 
     @pl.when(core == 1)
     def _():
-        total = [None, vec[...]]
+        total = [None, vec[chip]]
         for k in range(8):
             for c in range(2):
                 if (k, c) == (0, 1):
                     continue
                 remote(
-                    vec, ar1.at[k, c], a_send.at[k], a_recv.at[2 * k + c], seq_dev(1)
+                    ar1.at[k, c], ar1.at[k, c], a_send.at[k], a_recv.at[2 * k + c], seq_dev(1)
                 ).wait_recv()
                 total[c] = ar1[k, c] if total[c] is None else total[c] + ar1[k, c]
-        ar2[0, 0] = total[0]
-        ar2[0, 1] = total[1]
-        if near:
-            pl.semaphore_wait(barrier, len(near) + len(far))
-        for cp in near_step:
+        ar2[0, 0:1] = total[0]
+        ar2[0, 1:2] = total[1]
+        if pairs > 1:
+            pl.semaphore_wait(barrier, pairs - 1)
+        for cp in pair_step:
             cp.start()
+
 
     dq_far = remote(
         dqst.at[other], dq_hbm.at[:, own_cols], dq_sem.at[0], dq_sem.at[1], seq_dev(1)
@@ -464,16 +470,6 @@
     give(3, 9, 3)
     give(1, 10, 1)
 
-    @pl.when(core == 1)
-    def _():
-        total = ar2[0]
-        for k, cp in enumerate(near_step):
-            cp.wait_recv()
-            total = total + ar2[k + 1]
-        ar3[0] = total
-        for cp in far_step:
-            cp.start()
-
     add(8, 2, 4)
     give(8, 11, 8)
     add(9, 3, 5)
@@ -485,12 +481,13 @@
 
     @pl.when(core == 1)
     def _():
-        total = ar3[0]
-        for k, cp in enumerate(far_step):
-            cp.wait_recv()
-            total = total + ar3[k + 1]
-        res[...] = total
-        last.start()
+        total = ar2[0]
+        for n in range(1, pairs):
+            pair_step[n - 1].wait_recv()
+            total = total + ar2[n]
+        res[chip] = total
+        for cp in spread:
+            cp.start()
 
     mine = part(0)[...].astype(F32)
     for slot in (6, 11, 13):
@@ -504,14 +501,20 @@
         dkv_ref[:, pl.ds(pl.multiple_of(head * 128, 128), 128)] = value[:, :128]
         dkv_ref[:, pl.ds(pl.multiple_of(256 + head * 128, 128), 128)] = value[:, 128:]
 
+    def rows_from(k):
+        at = res.at[xor(s, 2 * k) // 2]
+        remote(at, at, c_send.at[k], c_recv.at[k], seq_dev(1)).wait_recv()
+
     @pl.when(core == 0)
     def _():
-        last.wait_recv()
-
+        rows_from(0)
+
+    for k in range(1, 8):
+        rows_from(k)
     for head in range(2):
         for h in range(HEADS):
-            bq_ref[pl.ds((head * HEADS + h) * DIM, DIM)] = res[head, h]
-        bv_ref[pl.ds(head * DIM, DIM)] = res[head, 7]
+            bq_ref[pl.ds((head * HEADS + h) * DIM, DIM)] = res[h, head]
+        bv_ref[pl.ds(head * DIM, DIM)] = res[7, head]
 
     dq_own.wait()
     dq_far.wait_recv()
@@ -527,7 +530,7 @@
 
     @pl.when(core == 1)
     def _():
-        for cp in near_step + far_step + [last]:
+        for cp in pair_step + spread:
             cp.wait_send()
 
 
@@ -541,8 +544,6 @@
 
 
 def on_device(pairs, queries, keys_values, cotangent, resp_len, query_bias):
-    near = [n for n in range(1, min(pairs, 4))]
-    far = [n for n in range(4, pairs, 4)]
     vm = pltpu.VMEM
     dma = pltpu.SemaphoreType.DMA
     any_spec = pl.BlockSpec(memory_space=pl.ANY)
@@ -579,11 +580,10 @@
         vm((UNITS, 4, 128, 256), BF16),
         vm((16, 128, 256), BF16),
         vm((2, 128, RLANES), F32),
-        vm((8, 128), F32),
-        vm((8, 2, 8, 128), F32),
-        vm((len(near) + 1, 2, 8, 128), F32),
-        vm((len(far) + 1, 2, 8, 128), F32),
-        vm((2, 8, 128), F32),
+        vm((8, 1, 128), F32),
+        vm((8, 2, 1, 128), F32),
+        vm((pairs, 2, 128), F32),
+        vm((8, 2, 128), F32),
         pltpu.SMEM((1, 2), jnp.int32),
         vm((2 * RLANES,), F32),
         dma((8,)),
@@ -594,9 +594,12 @@
         dma((16,)),
         dma((16,)),
         dma((3,)),
-        dma((19,)),
+        dma((8,)),
         dma((16,)),
-        dma((19,)),
+        dma((pairs,)),
+        dma((pairs,)),
+        dma((16,)),
+        dma((8,)),
         pltpu.SemaphoreType.REGULAR,
     ]
     shapes = (
@@ -606,7 +609,7 @@
         jax.ShapeDtypeStruct((256,), F32),
     )
     made = pl.pallas_call(
-        functools.partial(kernel, near, far),
+        functools.partial(kernel, pairs),
         out_shape=shapes,
         in_specs=[
             hbm_spec,

time: 51.1 us -> 49.8 us (0.975)
  Pallas kernels: 50.3 us -> 49 us
    pallas_call x1, Pallas kernels: 48 us -> 46.7 us  [on_device(): pl.pallas_call(functools.partial(kernel, pairs), out_shape=shapes, in_spe...]
where the time goes in v4:
time: 49.8 us; the launch traced here: 49.7 us
  Pallas kernels  49 us (98%)
  between operations  0.64 us (1%)
    pallas_call x1, Pallas kernels, on_device(): pl.pallas_call(functools.partial(kernel, pairs), out_shape=shapes, in_spe...  46.7 us
    pallas_call x1, Pallas kernels, on_device(): pl.pallas_call(hand_out, out_shape=shapes, in_specs=[vmem_spec] * 4, out_...  2.31 us

profile of v4, /device:TPU:1, one launch (start us, length us, event | category | flops | bytes accessed | tf_op | source)
XLA Modules:
  0.0 49.7 jit_solution(15077784140692477032)
XLA Ops:
  0.6 46.7 %shard_map.84 = (f32[128,1792]{1,0:T(8,128)}, f32[128,512]{1,0:T(8,128)}, f32[1792]{0:T(1024)}, f32[256]{0:T(256)}) custom-call(bf16[128,1792]{1,0:T(8,128)(2,1)} %bitcast.5, bf16[128,512]{1,0:T(8,128)(2,1)} %bitcast.7, bf16[128,1792]{1,0:T(8,128)(2,1)} %bitcast.6, s32[1,2]{1,0:T(1,128)} %len_hbm.1, f32[1792]{0:T(1024)} %bias_hbm.1), custom_call_target="tpu_custom_call" | custom-call | tf_op jit(solution)/shard_map/pallas_call | solution.py:611
  47.3 2.3 %shard_map.85 = (f32[128,1792]{1,0:T(8,128)}, f32[128,512]{1,0:T(8,128)}, f32[1792]{0:T(1024)}, f32[256]{0:T(256)}) custom-call(f32[128,1792]{1,0:T(8,128)} %get-tuple-element.12.refs_0_, f32[128,512]{1,0:T(8,128)} %get-tuple-element.13.refs_1_, f32[1792]{0:T(1024)} %get-tuple-element.14.refs_2_, f32[256]{0:T(256)} %get-tuple-element.15.refs_3_), custom_call_target="tpu_custom_call" | custom-call | tf_op jit(solution)/shard_map/pallas_call | solution.py:627

commit v5 on v4

--- a/solution.py
+++ b/solution.py
@@ -434,9 +434,6 @@
     give(10, 4, 2)
     give(11, 5, 2)
 
-    grad_kv(1)
-    give(6, 6, 6)
-
     @pl.when(core == 1)
     def _():
         total = [None, vec[chip]]
@@ -455,6 +452,8 @@
         for cp in pair_step:
             cp.start()
 
+    grad_kv(1)
+    give(6, 6, 6)
 
     dq_far = remote(
         dqst.at[other], dq_hbm.at[:, own_cols], dq_sem.at[0], dq_sem.at[1], seq_dev(1)
@@ -610,7 +609,7 @@
     )
     made = pl.pallas_call(
         functools.partial(kernel, pairs),
-        out_shape=shapes,
+        out_shape=tuple(pltpu.VMEM(a.shape, a.dtype) for a in shapes),
         in_specs=[
             hbm_spec,
             hbm_spec,
@@ -621,15 +620,16 @@
         out_specs=(any_spec, vmem_spec, vmem_spec, vmem_spec),
         scratch_shapes=scratch,
         compiler_params=pltpu.CompilerParams(
-            collective_id=0, has_side_effects=True, vmem_limit_bytes=63 * 1024 * 1024
+            collective_id=0, has_side_effects=True, vmem_limit_bytes=61 * 1024 * 1024
         ),
     )(queries[0], keys_values[0], cotangent[0], resp_len, query_bias)
     dq, dkv, bq, bv = pl.pallas_call(
         hand_out,
         out_shape=shapes,
-        in_specs=[vmem_spec] * 4,
+        in_specs=[any_spec] * 4,
         out_specs=(any_spec,) * 4,
         scratch_shapes=[dma((4,))],
+        compiler_params=pltpu.CompilerParams(vmem_limit_bytes=16 * 1024 * 1024),
     )(*made)
     return dq[None], dkv[None], bq, bv
 

time: 49.8 us -> 47.8 us (0.960)
  Pallas kernels: 49 us -> 47.1 us
    pallas_call x2, Pallas kernels: 49 us -> 47.1 us  [the longest x1 46 us: on_device(): pl.pallas_call(functools.partial(kernel, pairs), out_shape=tuple((pltpu.V...]
where the time goes in v5:
time: 47.8 us; the launch traced here: 47.7 us
  Pallas kernels  47.1 us (99%)
  between operations  0.64 us (1%)
    pallas_call x1, Pallas kernels, on_device(): pl.pallas_call(functools.partial(kernel, pairs), out_shape=tuple((pltpu.V...  46 us
    pallas_call x1, Pallas kernels, on_device(): pl.pallas_call(hand_out, out_shape=shapes, in_specs=[any_spec] * 4, out_s...  1.05 us

profile of v5, /device:TPU:1, one launch (start us, length us, event | category | flops | bytes accessed | tf_op | source)
XLA Modules:
  0.0 47.7 jit_solution(4189557657073050553)
XLA Ops:
  0.6 46.0 %shard_map.84 = (f32[128,1792]{1,0:T(8,128)S(1)}, f32[128,512]{1,0:T(8,128)S(1)}, f32[1792]{0:T(1024)S(1)}, f32[256]{0:T(256)S(1)}) custom-call(bf16[128,1792]{1,0:T(8,128)(2,1)} %bitcast.5, bf16[128,512]{1,0:T(8,128)(2,1)} %bitcast.7, bf16[128,1792]{1,0:T(8,128)(2,1)} %bitcast.6, s32[1,2]{1,0:T(1,128)} %len_hbm.1, f32[1792]{0:T(1024)} %bias_hbm.1), custom_call_target="tpu_custom_call" | custom-call | tf_op jit(solution)/shard_map/pallas_call | solution.py:610
  46.6 1.0 %shard_map.85 = (f32[128,1792]{1,0:T(8,128)}, f32[128,512]{1,0:T(8,128)}, f32[1792]{0:T(1024)}, f32[256]{0:T(256)}) custom-call(f32[128,1792]{1,0:T(8,128)S(1)} %get-tuple-element.12.refs_0_, f32[128,512]{1,0:T(8,128)S(1)} %get-tuple-element.13.refs_1_, f32[1792]{0:T(1024)S(1)} %get-tuple-element.14.refs_2_, f32[256]{0:T(256)S(1)} %get-tuple-element.15.refs_3_), custom_call_target="tpu_custom_call" | custom-call | tf_op jit(solution)/shard_map/pallas_call | solution.py:626

commit v6 on v5

--- a/solution.py
+++ b/solution.py
@@ -393,13 +393,7 @@
                 dqst[blk, 64:96, cols] = right[32 * blk : 32 * blk + 32]
                 dqst[blk, 96:128, cols] = right[64 + 32 * blk : 96 + 32 * blk]
 
-    grad_scores(3)
-    grad_kv(3)
-    give(12, 0, 8)
-    give(14, 2, 6)
-    give(13, 1, 8)
-    give(15, 3, 6)
-    for u in (2, 1, 0):
+    for u in reversed(range(UNITS)):
         grad_scores(u)
     grad_queries()
     vec[7] = dot(jnp.ones((8, LANES), BF16), docat[...])[0:1]
@@ -430,9 +424,11 @@
         for m in range(1, 16)
     ]
 
-    grad_kv(2)
-    give(10, 4, 2)
-    give(11, 5, 2)
+    grad_kv(3)
+    give(12, 0, 8)
+    give(14, 2, 6)
+    give(13, 1, 8)
+    give(15, 3, 6)
 
     @pl.when(core == 1)
     def _():
@@ -451,6 +447,10 @@
             pl.semaphore_wait(barrier, pairs - 1)
         for cp in pair_step:
             cp.start()
+
+    grad_kv(2)
+    give(10, 4, 2)
+    give(11, 5, 2)
 
     grad_kv(1)
     give(6, 6, 6)

time: 47.8 us -> 47.3 us (0.990)
  Pallas kernels: 47.1 us -> 46.5 us
    pallas_call x1, Pallas kernels: 46 us -> 45.5 us  [on_device(): pl.pallas_call(functools.partial(kernel, pairs), out_shape=tuple((pltpu.V...]
where the time goes in v6:
time: 47.3 us; the launch traced here: 47.2 us
  Pallas kernels  46.5 us (98%)
  between operations  0.64 us (1%)
    pallas_call x1, Pallas kernels, on_device(): pl.pallas_call(functools.partial(kernel, pairs), out_shape=tuple((pltpu.V...  45.5 us
    pallas_call x1, Pallas kernels, on_device(): pl.pallas_call(hand_out, out_shape=shapes, in_specs=[any_spec] * 4, out_s...  1.05 us

profile of v6, /device:TPU:1, one launch (start us, length us, event | category | flops | bytes accessed | tf_op | source)
XLA Modules:
  0.0 47.2 jit_solution(10664827233182510458)
XLA Ops:
  0.6 45.5 %shard_map.84 = (f32[128,1792]{1,0:T(8,128)S(1)}, f32[128,512]{1,0:T(8,128)S(1)}, f32[1792]{0:T(1024)S(1)}, f32[256]{0:T(256)S(1)}) custom-call(bf16[128,1792]{1,0:T(8,128)(2,1)} %bitcast.5, bf16[128,512]{1,0:T(8,128)(2,1)} %bitcast.7, bf16[128,1792]{1,0:T(8,128)(2,1)} %bitcast.6, s32[1,2]{1,0:T(1,128)} %len_hbm.1, f32[1792]{0:T(1024)} %bias_hbm.1), custom_call_target="tpu_custom_call" | custom-call | tf_op jit(solution)/shard_map/pallas_call | solution.py:610
  46.1 1.0 %shard_map.85 = (f32[128,1792]{1,0:T(8,128)}, f32[128,512]{1,0:T(8,128)}, f32[1792]{0:T(1024)}, f32[256]{0:T(256)}) custom-call(f32[128,1792]{1,0:T(8,128)S(1)} %get-tuple-element.12.refs_0_, f32[128,512]{1,0:T(8,128)S(1)} %get-tuple-element.13.refs_1_, f32[1792]{0:T(1024)S(1)} %get-tuple-element.14.refs_2_, f32[256]{0:T(256)S(1)} %get-tuple-element.15.refs_3_), custom_call_target="tpu_custom_call" | custom-call | tf_op jit(solution)/shard_map/pallas_call | solution.py:626
